TPU v7x, 32 devices: a whole 2x2x4 slice. The times are simulated.
32 devices in a mesh: grp: 2 (over y), seq: 4 (over z), head: 2 (over x), sub: 2 (over core).
Axes of the slice: x: 2, y: 2, z: 4, core: 2. Of those that a mesh axis runs over, the one named last changes fastest.
Arguments:
- tokens: bfloat16 [4096, 3584], P(('grp', 'seq', 'sub')), parts along dimension 0, may hold values from -12 to 12, as said below
- norm_gain: float32 [2, 3584], replicated, may hold values from 0.1 to 1.9
- w_query: bfloat16 [2, 3584, 2048], P(None, ('seq', 'sub'), 'head'), may hold values from -1 to 1
- w_key: bfloat16 [2, 3584, 512], P(None, ('seq', 'sub')), may hold values from -4 to 4
- w_value: bfloat16 [2, 3584, 512], P(None, ('seq', 'sub')), may hold values from -0.09375 to 0.09375
- w_out: bfloat16 [2, 2048, 3584], P(None, 'head', ('seq', 'sub')), may hold values from -0.125 to 0.125
- modality: int32 [4096], P('grp'), parts along dimension 0, may hold values from 0 to 1, as said below
- doc_ids: int32 [4096], P('grp'), parts along dimension 0, may hold values from 0 to 3, never falling along the last dimension, each value on 1 to 1536 neighbouring positions
Outputs:
- mixed: bfloat16 [4096, 3584], P(('grp', 'seq', 'sub'), 'head'), parts along dimension 0
There are 2 independent parts, one for each index of `grp`. A program takes and returns all parts, laid end to end along the dimension named above; an argument that names none is the same for every part. Nothing has to cross between parts.
Inputs may be any that keep to these rules, and one draw needn't show every extreme that they name: `tokens`: rows carry their own scale. `modality`: positions below 512 are 0; after that, each aligned run of 64 positions is all 0 or all 1. `doc_ids`: never falling along the positions; a document holds at most 1536 positions, and one holds exactly that many.
All inputs are finite; a program needn't handle non-finite values.
Results may differ from a plain program's by a relative error of at most 0.015.
Values may be sent and summed in bfloat16 or wider, within the bound.
A program may use at most 128 MiB of HBM per device.

v0:
```python
import math

import jax
import jax.numpy as jnp
from jax import lax
from jax.sharding import PartitionSpec as P

HEAD_DIM = 128
KV_HEADS = 4


EPS = 1e-06


def block_ids(modality, doc_ids):
    changed = (modality[1:] != modality[:-1]) | (doc_ids[1:] != doc_ids[:-1])
    begins = jnp.concatenate([jnp.ones((1,), jnp.int32), changed.astype(jnp.int32)])
    return jnp.cumsum(begins)


def body(tokens, norm_gain, w_query, w_key, w_value, w_out, modality, doc_ids):
    length = tokens.shape[0]
    head_count = lax.axis_size("head")
    head_index = lax.axis_index("head")
    first_pos = lax.axis_index(("seq", "sub")) * length
    blocks = block_ids(modality, doc_ids)
    own_mod = lax.dynamic_slice_in_dim(modality, first_pos, length)
    own_doc = lax.dynamic_slice_in_dim(doc_ids, first_pos, length)
    own_block = lax.dynamic_slice_in_dim(blocks, first_pos, length)
    generate = (own_mod == 1)[:, None]
    kv_local = max(KV_HEADS // head_count, 1)
    kv_first = head_index * KV_HEADS // head_count
    key_cols = lax.dynamic_slice_in_dim(w_key, kv_first * HEAD_DIM, kv_local * HEAD_DIM, 2)
    value_cols = lax.dynamic_slice_in_dim(w_value, kv_first * HEAD_DIM, kv_local * HEAD_DIM, 2)
    values32 = tokens.astype(jnp.float32)
    factor = lax.rsqrt(jnp.mean(values32 * values32, axis=1, keepdims=True) + EPS)
    gain = jnp.where(generate, norm_gain[1][None, :], norm_gain[0][None, :])
    normed = (values32 * factor * gain).astype(jnp.bfloat16)
    empty = tuple(
        (
            jnp.zeros((2, length, weight.shape[2]), jnp.float32)
            for weight in (w_query, key_cols, value_cols)
        )
    )
    pieces = (
        lax.all_gather(w_query, ("seq", "sub"), axis=1, tiled=True),
        lax.all_gather(key_cols, ("seq", "sub"), axis=1, tiled=True),
        lax.all_gather(value_cols, ("seq", "sub"), axis=1, tiled=True),
    )
    updated = []
    for summed, piece in zip(empty, pieces):
        first = jnp.dot(normed, piece[0], preferred_element_type=jnp.float32)
        second = jnp.dot(normed, piece[1], preferred_element_type=jnp.float32)
        updated.append(jnp.stack([first, second]))
    projected = tuple(updated)

    def select(both):
        return jnp.where(generate, both[1], both[0]).astype(jnp.bfloat16)

    query = select(projected[0])
    stacked = jnp.stack([select(projected[1]), select(projected[2])])
    q_local = query.shape[1] // HEAD_DIM
    repeat = q_local // kv_local
    grouped = query.reshape(length, kv_local, repeat, HEAD_DIM)
    query_pos = first_pos + jnp.arange(length, dtype=jnp.int32)
    root = math.sqrt(HEAD_DIM)

    def visit(carry, key_value, key_start):
        count = key_value.shape[1]
        key_doc = lax.dynamic_slice_in_dim(doc_ids, key_start, count)
        key_block = lax.dynamic_slice_in_dim(blocks, key_start, count)
        key_pos = key_start + jnp.arange(count, dtype=jnp.int32)
        seen = (own_doc[:, None] == key_doc[None, :]) & (
            (key_pos[None, :] <= query_pos[:, None])
            | (own_block[:, None] == key_block[None, :]) & (own_mod[:, None] == 1)
        )
        highest, weight_sum, summed = carry
        keys_here = key_value[0].reshape(count, kv_local, HEAD_DIM)
        values_here = key_value[1].reshape(count, kv_local, HEAD_DIM)
        scores = (
            jnp.einsum("qgrd,kgd->grqk", grouped, keys_here, preferred_element_type=jnp.float32)
            / root
        )
        scores = jnp.where(seen, scores, -1e30)
        new_high = jnp.maximum(highest, jnp.max(scores, axis=3))
        weights = jnp.where(seen, jnp.exp(scores - new_high[..., None]), 0.0)
        scaling = jnp.exp(highest - new_high)
        weight_sum = weight_sum * scaling + jnp.sum(weights, axis=3)
        probs = weights.astype(jnp.bfloat16)
        summed = summed * scaling[..., None] + jnp.einsum(
            "grqk,kgd->grqd", probs, values_here, preferred_element_type=jnp.float32
        )
        return (new_high, weight_sum, summed)

    start_state = (
        jnp.full((kv_local, repeat, length), -1e30, jnp.float32),
        jnp.zeros((kv_local, repeat, length), jnp.float32),
        jnp.zeros((kv_local, repeat, length, HEAD_DIM), jnp.float32),
    )
    piece = lax.all_gather(stacked, ("seq", "sub"), axis=1, tiled=True)
    count = piece.shape[1]
    step_size = math.gcd(count, 1024)

    def advance(number, state):
        offset = number * step_size
        portion = lax.dynamic_slice_in_dim(piece, offset, step_size, 1)
        return visit(state, portion, offset)

    final_state = lax.fori_loop(0, count // step_size, advance, start_state)
    attended = final_state[2] / final_state[1][..., None]
    attended = (
        jnp.transpose(attended, (2, 0, 1, 3))
        .reshape(length, q_local * HEAD_DIM)
        .astype(jnp.bfloat16)
    )
    out_piece = lax.all_gather(w_out, ("seq", "sub"), axis=2, tiled=True)
    first = jnp.dot(attended, out_piece[0], preferred_element_type=jnp.float32)
    second = jnp.dot(attended, out_piece[1], preferred_element_type=jnp.float32)
    partial_sum = jnp.where(generate, second, first).astype(jnp.bfloat16).astype(jnp.float32)
    reduced = lax.psum_scatter(
        partial_sum.astype(jnp.bfloat16), "head", scatter_dimension=1, tiled=True
    )
    return reduced


def solution(mesh):
    placed = (
        P(("grp", "seq", "sub"), None),
        P(),
        P(None, ("seq", "sub"), "head"),
        P(None, ("seq", "sub"), None),
        P(None, ("seq", "sub"), None),
        P(None, "head", ("seq", "sub")),
        P("grp"),
        P("grp"),
    )
    return jax.shard_map(
        body,
        mesh=mesh,
        in_specs=placed,
        out_specs=P(("grp", "seq", "sub"), "head"),
        check_vma=False,
    )
```

profile of v0, /device:TPU:0, one launch (start us, length us, event | category | flops | bytes accessed | tf_op | source)
XLA Modules:
  0.0 441.6 jit_solution(565932314161876169)
XLA Ops:
  6.6 1.1 copy-done
  7.7 0.8 constant_dynamic-slice_fusion.3
  8.6 1.8 constant_dynamic-slice_fusion.2
  10.5 0.7 all-gather.12.cloned.1.call-update
  11.2 0.1 broadcast_compare_fusion.1
  11.4 0.4 fusion.21
  11.9 42.5 %all-gather.6.cloned.1.call-done = bf16[2,3584,256]{2,1,0:T(8,128)(2,1)} async-done(((bf16[2,448,256]{2,1,0:T(8,128)(2,1)}), bf16[2,3584,256]{2,1,0:T(8,128)(2,1)}) %all-gather.6.cloned.1.call-update) | async-done | bytes 3670032 | tf_op jit(solution)/shard_map/all_gather | solution.py:47
  54.3 2.2 fusion.26
  56.6 40.8 %all-gather.8.cloned.1.call-done = bf16[2,3584,256]{2,1,0:T(8,128)(2,1)} async-done(((bf16[2,448,256]{2,1,0:T(8,128)(2,1)}), bf16[2,3584,256]{2,1,0:T(8,128)(2,1)}) %all-gather.8.cloned.1.call-update) | async-done | bytes 3670032 | tf_op jit(solution)/shard_map/all_gather | solution.py:48
  97.4 2.4 fusion.24
  99.8 0.2 copy-done.7
  100.0 0.8 fusion.34
  100.8 1.3 copy-done.8
  102.0 0.8 fusion.35
  102.8 0.7 pad_maximum_fusion
  103.6 0.5 all-gather.14.cloned.1.call-update
  104.3 0.1 dynamic_slice.37
  104.3 0.1 fusion.36
  104.4 0.1 convert_bitcast_fusion
  104.5 0.3 reduce-window.9
  104.9 0.1 slice_reduce_fusion.2
  105.2 126.7 %all-gather.12.cloned.1.call-done = bf16[2,3584,1024]{2,1,0:T(8,128)(2,1)} async-done(((bf16[2,448,1024]{2,1,0:T(8,128)(2,1)}), bf16[2,3584,1024]{2,1,0:T(8,128)(2,1)}) %all-gather.12.cloned.1.call-update) | async-done | bytes 14680080 | tf_op jit(solution)/shard_map/all_gather | solution.py:46
  231.9 5.3 %fusion.17 = bf16[256,1024]{1,0:T(8,128)(2,1)S(1)} fusion(bf16[2,3584,1024]{2,1,0:T(8,128)(2,1)} %all-gather.12.cloned.1.call-done, bf16[256,3584]{1,0:T(8,128)(2,1)S(1)} %copy-done.2, f32[3584]{0:T(1024)S(1)} %get-tuple-element.274, f32[3584]{0:T(1024)S(1)} %get-tuple-element.273, f32[256]{0:T(256)S(1)} %add_rsqrt_fusion, ...), kind=kOutput, calls=%fused_computation.28 | convolution fusion | flops 1883635712 | bytes 9729280 | tf_op jit(solution)/shard_map/dot_general | solution.py:52
  237.2 2.1 copy-done.6
  239.3 2.2 fusion.29
  241.5 0.4 reshape.50
  241.9 18.7 %all-gather.10.cloned.1.call-done = bf16[2,2048,256]{2,1,0:T(8,128)(2,1)} async-done(((bf16[2,256,256]{2,1,0:T(8,128)(2,1)}), bf16[2,2048,256]{2,1,0:T(8,128)(2,1)}) %all-gather.10.cloned.1.call-update) | async-done | bytes 2097168 | tf_op jit(solution)/shard_map/all_gather | solution.py:100
  260.6 39.9 %while.18 = (s32[]{:T(128)}, f32[2,4,256]{2,1,0:T(4,128)S(1)}, f32[2,4,256]{2,1,0:T(4,128)S(1)}, f32[2,4,256,128]{3,2,1,0:T(8,128)}, s32[256]{0:T(256)S(1)}, /*i...) while((s32[]{:T(128)}, f32[2,4,256]{2,1,0:T(4,128)S(1)}, ...), condition=%wide.region_6.7_spmd.clone, body=%wide.region_3.6_spmd.clone.sunk | while | flops 1103375872 | bytes 34248440 | solution.py:109
  260.7 0.9 or_and_fusion.2
  261.6 1.3 constant_dynamic-slice_fusion.5
  262.9 0.2 copy.29
  263.1 4.8 %fusion.60 = (f32[2,4,256]{2,1,0:T(4,128)S(1)}, f32[2,1024,256,4]{2,1,3,0:T(8,128)}) fusion(pred[256,1024]{0,1:T(8,128)(4,1)S(1)} %or_and_fusion.2, bf16[1024,2,128,1]{0,2,3,1:T(8,128)(2,1)S(1)} %bitcast.99, bf16[256,2,4,128]{3,0,2,1:T(8,128)(2,1)S(1)} %get-tuple-element.436), kind=kOutput, calls=%fused_computation.3.clone.1 | convolution fusion | flops 543160320 | bytes 9707520 | tf_op jit(solution)/shard_map/while/body/eval_jaxpr/qgrd,kgd->grqk/dot_general | solution.py:81
  267.9 5.5 %fusion.61 = f32[2,4,256]{2,1,0:T(4,128)S(1)} fusion(f32[2,1024,256,4]{2,1,3,0:T(8,128)} %get-tuple-element.388, f32[2,4,256]{2,1,0:T(4,128)S(1)} %select_maximum_fusion.2, pred[256,1024]{0,1:T(8,128)(4,1)S(1)} %or_and_fusion.2), kind=kLoop, calls=%fused_computation.5.clone.1 | loop fusion | flops 10483712 | bytes 8667136 | tf_op jit(solution)/shard_map/while/body/eval_jaxpr/reduce_sum | solution.py:88
  273.5 0.2 copy.30
  273.7 7.3 %fusion.63 = f32[2,4,256,128]{3,2,1,0:T(8,128)} fusion(bf16[1024,2,128,1]{0,2,3,1:T(8,128)(2,1)S(1)} %bitcast.100, f32[2,1024,256,4]{2,1,3,0:T(8,128)} %get-tuple-element.388, f32[2,4,256]{2,1,0:T(4,128)S(1)} %select_maximum_fusion.2, pred[256,1024]{0,1:T(8,128)(4,1)S(1)} %or_and_fusion.2, f32[2,4,256,128]{3,2,1,0:T(8,128)} %get-tuple-element.412, ...), kind=kOutput, calls=%fused_computation.8.clone.1 | convolution fusion | flops 548143104 | bytes 11288577 | tf_op jit(solution)/shard_map/while/body/eval_jaxpr/grqk,kgd->grqd/dot_general | solution.py:90
  281.0 0.9 or_and_fusion.2
  281.9 1.3 constant_dynamic-slice_fusion.5
  283.2 0.2 copy.29
  283.4 4.8 %fusion.60 = (f32[2,4,256]{2,1,0:T(4,128)S(1)}, f32[2,1024,256,4]{2,1,3,0:T(8,128)}) fusion(pred[256,1024]{0,1:T(8,128)(4,1)S(1)} %or_and_fusion.2, bf16[1024,2,128,1]{0,2,3,1:T(8,128)(2,1)S(1)} %bitcast.99, bf16[256,2,4,128]{3,0,2,1:T(8,128)(2,1)S(1)} %get-tuple-element.436), kind=kOutput, calls=%fused_computation.3.clone.1 | convolution fusion | flops 543160320 | bytes 9707520 | tf_op jit(solution)/shard_map/while/body/eval_jaxpr/qgrd,kgd->grqk/dot_general | solution.py:81
  288.3 4.6 %fusion.61 = f32[2,4,256]{2,1,0:T(4,128)S(1)} fusion(f32[2,1024,256,4]{2,1,3,0:T(8,128)} %get-tuple-element.388, f32[2,4,256]{2,1,0:T(4,128)S(1)} %select_maximum_fusion.2, pred[256,1024]{0,1:T(8,128)(4,1)S(1)} %or_and_fusion.2), kind=kLoop, calls=%fused_computation.5.clone.1 | loop fusion | flops 10483712 | bytes 8667136 | tf_op jit(solution)/shard_map/while/body/eval_jaxpr/reduce_sum | solution.py:88
  292.9 0.2 copy.30
  293.1 7.5 %fusion.63 = f32[2,4,256,128]{3,2,1,0:T(8,128)} fusion(bf16[1024,2,128,1]{0,2,3,1:T(8,128)(2,1)S(1)} %bitcast.100, f32[2,1024,256,4]{2,1,3,0:T(8,128)} %get-tuple-element.388, f32[2,4,256]{2,1,0:T(4,128)S(1)} %select_maximum_fusion.2, pred[256,1024]{0,1:T(8,128)(4,1)S(1)} %or_and_fusion.2, f32[2,4,256,128]{3,2,1,0:T(8,128)} %get-tuple-element.412, ...), kind=kOutput, calls=%fused_computation.8.clone.1 | convolution fusion | flops 548143104 | bytes 11288577 | tf_op jit(solution)/shard_map/while/body/eval_jaxpr/grqk,kgd->grqd/dot_general | solution.py:90
  300.6 1.6 copy.16
  302.2 0.1 divide_convert_fusion
  302.3 93.3 %all-gather.14.cloned.1.call-done = bf16[2,1024,3584]{1,2,0:T(8,128)(2,1)} async-done(((bf16[2,1024,448]{1,2,0:T(8,128)(2,1)}), bf16[2,1024,3584]{1,2,0:T(8,128)(2,1)}) %all-gather.14.cloned.1.call-update) | async-done | bytes 14680080 | tf_op jit(solution)/shard_map/all_gather | solution.py:116
  395.5 5.2 %fusion.15 = bf16[256,3584]{1,0:T(8,128)(2,1)S(1)} fusion(bf16[256,1024]{0,1:T(8,128)(2,1)S(1)} %bitcast.101, bf16[2,1024,3584]{1,2,0:T(8,128)(2,1)} %all-gather.14.cloned.1.call-done), kind=kOutput, calls=%fused_computation.24 | convolution fusion | flops 1879048192 | bytes 9699328 | tf_op jit(solution)/shard_map/dot_general | solution.py:117
  400.8 6.7 %fusion.20 = bf16[256,3584]{1,0:T(8,128)(2,1)} fusion(bf16[256,3584]{1,0:T(8,128)(2,1)S(1)} %fusion.15, bf16[256,1024]{0,1:T(8,128)(2,1)S(1)} %bitcast.102, bf16[2,1024,3584]{1,2,0:T(8,128)(2,1)} %all-gather.14.cloned.1.call-done, pred[256]{0:T(512)(128)(4,1)S(1)} %get-tuple-element.301), kind=kOutput, calls=%fused_computation.32 | convolution fusion | flops 1879965696 | bytes 11534592 | tf_op jit(solution)/shard_map/dot_general | solution.py:118
  407.5 27.3 %reduce-scatter.2.cloned.1.call-done = bf16[256,1792]{1,0:T(8,128)(2,1)} async-done(((bf16[256,3584]{1,0:T(8,128)(2,1)}), bf16[256,1792]{1,0:T(8,128)(2,1)}) %reduce-scatter.2.cloned.1.call-update) | async-done | bytes 917520 | tf_op jit(solution)/shard_map/reduce_scatter | solution.py:120
  (50 shorter events, 0.8 us)
Async XLA Ops:
  6.5 1.2 copy-start
  6.5 4.7 %copy-start.4 = (s32[2048]{0:T(1024)S(1)}, s32[2048]{0:T(1024)}, u32[]{:S(2)}) copy-start(s32[2048]{0:T(1024)} %param.16) | copy-start | bytes 24580
  6.5 4.8 %copy-start.5 = (f32[2,3584]{1,0:T(2,128)S(1)}, f32[2,3584]{1,0:T(2,128)}, u32[]{:S(2)}) copy-start(f32[2,3584]{1,0:T(2,128)} %param.11) | copy-start | bytes 86020
  6.5 4.9 %copy-start.2 = (bf16[256,3584]{1,0:T(8,128)(2,1)S(1)}, bf16[256,3584]{1,0:T(8,128)(2,1)}, u32[]{:S(2)}) copy-start(bf16[256,3584]{1,0:T(8,128)(2,1)} %param.10) | copy-start | bytes 5505028
  6.5 47.8 %all-gather.6.cloned.1.call-start = ((), (), s32[]{:S(2)}) async-start(), calls=%async_computation.1 | async-start | bytes 4128768 | tf_op jit(solution)/shard_map/all_gather | solution.py:47
  8.5 88.9 %all-gather.8.cloned.1.call-start = ((), (), s32[]{:S(2)}) async-start(), calls=%async_computation.2 | async-start | bytes 4128768 | tf_op jit(solution)/shard_map/all_gather | solution.py:48
  10.4 221.4 %all-gather.12.cloned.1.call-start = ((), (), s32[]{:S(2)}) async-start(), calls=%async_computation.4 | async-start | bytes 16515072 | tf_op jit(solution)/shard_map/all_gather | solution.py:46
  11.2 249.5 %all-gather.10.cloned.1.call-start = ((), (), s32[]{:S(2)}) async-start(), calls=%async_computation.3 | async-start | bytes 2359296 | tf_op jit(solution)/shard_map/all_gather | solution.py:100
  97.4 2.6 copy-start.7
  100.0 2.0 copy-start.8
  102.0 2.2 copy-start.3
  103.6 292.0 %all-gather.14.cloned.1.call-start = ((), (), s32[]{:S(2)}) async-start(), calls=%async_computation.5 | async-start | bytes 16515072 | tf_op jit(solution)/shard_map/all_gather | solution.py:116
  104.2 330.6 %reduce-scatter.2.cloned.1.call-start = ((), (), s32[]{:S(2)}) async-start(), calls=%async_computation.6 | async-start | bytes 2752512 | tf_op jit(solution)/shard_map/reduce_scatter | solution.py:120
  231.9 7.4 %copy-start.6 = (bf16[2,3584,1024]{2,1,0:T(8,128)(2,1)S(1)}, bf16[2,3584,1024]{2,1,0:T(8,128)(2,1)}, u32[]{:S(2)}) copy-start(bf16[2,3584,1024]{2,1,0:T(8,128)(2,1)} %all-gather.12.cloned.1.call-done) | copy-start | bytes 44040196
  400.8 34.0 %copy-start.1 = (bf16[2,448,512]{2,1,0:T(8,128)(2,1)S(1)}, bf16[2,448,512]{2,1,0:T(8,128)(2,1)}, u32[]{:S(2)}) copy-start(bf16[2,448,512]{2,1,0:T(8,128)(2,1)} %param.13) | copy-start | bytes 2752516
Sparse Core Ops, SparseCore 0:
  9.0 45.2 all-gather.5
  55.9 41.4 all-gather.7
  99.0 132.7 all-gather.11
  233.3 27.2 all-gather.9
  262.1 133.4 all-gather.13
  407.6 27.1 reduce-scatter.1
where the time goes:
time: 442 us
  waiting for transfers between devices  351 us (79%)
  matrix products  50.1 us (11%)
  other arithmetic  14 us (3%)
  between operations  13.7 us (3%)
  local copies, waits for them, and re-layouts  13 us (3%)
    all_gather x1, waiting for transfers between devices, body(): lax.all_gather(w_query, ('seq', 'sub'), axis=1, tiled=True)  127 us
    all_gather x1, waiting for transfers between devices, body(): out_piece = lax.all_gather(w_out, ('seq', 'sub'), axis=2, tiled=True)  93.3 us
    all_gather x1, waiting for transfers between devices, body(): lax.all_gather(key_cols, ('seq', 'sub'), axis=1, tiled=True)  42.5 us
    all_gather x1, waiting for transfers between devices, body(): lax.all_gather(value_cols, ('seq', 'sub'), axis=1, tiled=True)  40.8 us
    reduce_scatter x1, waiting for transfers between devices, body(): lax.psum_scatter(partial_sum.astype(jnp.bfloat16), 'head', scatter_dimens...  27.3 us
    all_gather x1, waiting for transfers between devices, body(): piece = lax.all_gather(stacked, ('seq', 'sub'), axis=1, tiled=True)  18.7 us
    dot_general x2, matrix products, visit(): jnp.einsum('grqk,kgd->grqd', probs, values_here, preferred_element_type=j...  14.8 us
    reduce_sum x2, other arithmetic, visit(): weight_sum = weight_sum * scaling + jnp.sum(weights, axis=3)  10.2 us
  transfers between devices with their start and end apart: 6, of which 6 were waited for; matrix products, arithmetic and copies ran while one was open for 14% of the time, Pallas kernels for 0%

commit v1 on v0

--- a/solution.py
+++ b/solution.py
@@ -18,6 +18,15 @@
     return jnp.cumsum(begins)
 
 
+def gather_weight(shard):
+    both, _, columns = shard.shape
+    if lax.axis_size("grp") != both:
+        return lax.all_gather(shard, ("seq", "sub"), axis=1, tiled=True)
+    own = lax.dynamic_index_in_dim(shard, lax.axis_index("grp"), 0, keepdims=False)
+    whole = lax.all_gather(own, ("grp", "seq", "sub"), axis=0, tiled=True)
+    return whole.reshape(both, -1, columns)
+
+
 def body(tokens, norm_gain, w_query, w_key, w_value, w_out, modality, doc_ids):
     length = tokens.shape[0]
     head_count = lax.axis_size("head")
@@ -36,29 +45,18 @@
     factor = lax.rsqrt(jnp.mean(values32 * values32, axis=1, keepdims=True) + EPS)
     gain = jnp.where(generate, norm_gain[1][None, :], norm_gain[0][None, :])
     normed = (values32 * factor * gain).astype(jnp.bfloat16)
-    empty = tuple(
-        (
-            jnp.zeros((2, length, weight.shape[2]), jnp.float32)
-            for weight in (w_query, key_cols, value_cols)
-        )
-    )
-    pieces = (
-        lax.all_gather(w_query, ("seq", "sub"), axis=1, tiled=True),
-        lax.all_gather(key_cols, ("seq", "sub"), axis=1, tiled=True),
-        lax.all_gather(value_cols, ("seq", "sub"), axis=1, tiled=True),
-    )
-    updated = []
-    for summed, piece in zip(empty, pieces):
-        first = jnp.dot(normed, piece[0], preferred_element_type=jnp.float32)
-        second = jnp.dot(normed, piece[1], preferred_element_type=jnp.float32)
-        updated.append(jnp.stack([first, second]))
-    projected = tuple(updated)
+    key_value_weight = jnp.concatenate([key_cols, value_cols], axis=2)
+    kv_both = gather_weight(key_value_weight)
+    q_both = gather_weight(w_query)
+    out_both = gather_weight(jnp.swapaxes(w_out, 1, 2))
 
-    def select(both):
-        return jnp.where(generate, both[1], both[0]).astype(jnp.bfloat16)
+    def project(both):
+        first = jnp.dot(normed, both[0], preferred_element_type=jnp.float32)
+        second = jnp.dot(normed, both[1], preferred_element_type=jnp.float32)
+        return jnp.where(generate, second, first).astype(jnp.bfloat16)
 
-    query = select(projected[0])
-    stacked = jnp.stack([select(projected[1]), select(projected[2])])
+    stacked = project(kv_both)
+    query = project(q_both)
     q_local = query.shape[1] // HEAD_DIM
     repeat = q_local // kv_local
     grouped = query.reshape(length, kv_local, repeat, HEAD_DIM)
@@ -66,7 +64,7 @@
     root = math.sqrt(HEAD_DIM)
 
     def visit(carry, key_value, key_start):
-        count = key_value.shape[1]
+        count = key_value.shape[0]
         key_doc = lax.dynamic_slice_in_dim(doc_ids, key_start, count)
         key_block = lax.dynamic_slice_in_dim(blocks, key_start, count)
         key_pos = key_start + jnp.arange(count, dtype=jnp.int32)
@@ -75,8 +73,8 @@
             | (own_block[:, None] == key_block[None, :]) & (own_mod[:, None] == 1)
         )
         highest, weight_sum, summed = carry
-        keys_here = key_value[0].reshape(count, kv_local, HEAD_DIM)
-        values_here = key_value[1].reshape(count, kv_local, HEAD_DIM)
+        keys_here = key_value[:, : kv_local * HEAD_DIM].reshape(count, kv_local, HEAD_DIM)
+        values_here = key_value[:, kv_local * HEAD_DIM :].reshape(count, kv_local, HEAD_DIM)
         scores = (
             jnp.einsum("qgrd,kgd->grqk", grouped, keys_here, preferred_element_type=jnp.float32)
             / root
@@ -97,13 +95,13 @@
         jnp.zeros((kv_local, repeat, length), jnp.float32),
         jnp.zeros((kv_local, repeat, length, HEAD_DIM), jnp.float32),
     )
-    piece = lax.all_gather(stacked, ("seq", "sub"), axis=1, tiled=True)
-    count = piece.shape[1]
+    piece = lax.all_gather(stacked, ("seq", "sub"), axis=0, tiled=True)
+    count = piece.shape[0]
     step_size = math.gcd(count, 1024)
 
     def advance(number, state):
         offset = number * step_size
-        portion = lax.dynamic_slice_in_dim(piece, offset, step_size, 1)
+        portion = lax.dynamic_slice_in_dim(piece, offset, step_size, 0)
         return visit(state, portion, offset)
 
     final_state = lax.fori_loop(0, count // step_size, advance, start_state)
@@ -113,9 +111,9 @@
         .reshape(length, q_local * HEAD_DIM)
         .astype(jnp.bfloat16)
     )
-    out_piece = lax.all_gather(w_out, ("seq", "sub"), axis=2, tiled=True)
-    first = jnp.dot(attended, out_piece[0], preferred_element_type=jnp.float32)
-    second = jnp.dot(attended, out_piece[1], preferred_element_type=jnp.float32)
+    contract = (((1,), (1,)), ((), ()))
+    first = lax.dot_general(attended, out_both[0], contract, preferred_element_type=jnp.float32)
+    second = lax.dot_general(attended, out_both[1], contract, preferred_element_type=jnp.float32)
     partial_sum = jnp.where(generate, second, first).astype(jnp.bfloat16).astype(jnp.float32)
     reduced = lax.psum_scatter(
         partial_sum.astype(jnp.bfloat16), "head", scatter_dimension=1, tiled=True

time: 442 us -> 386 us (0.87)
  waiting for transfers between devices: 351 us -> 299 us
  matrix products: 50.1 us -> 45.3 us
    all_gather x5 -> x4, waiting for transfers between devices: 322 us -> 272 us  [the longest x3 253 us: gather_weight(): whole = lax.all_gather(own, ('grp', 'seq', 'sub'), axis=0, tiled=True)]
    dot_general x2, matrix products: 14.8 us -> 10.3 us  [visit(): jnp.einsum('grqk,kgd->grqd', probs, values_here, preferred_element_type=j...]
    dot_general x8 -> x6, matrix products: 25.7 us -> 25.4 us  [the longest x2 9.26 us: project(): first = jnp.dot(normed, both[0], preferred_element_type=jnp.float32)]
  transfers between devices with their start and end apart: 6 -> 5, of which waited for: 6 -> 5; matrix products, arithmetic and copies ran while one was open for 14% -> 14% of each run, Pallas kernels for 0% -> 0%
where the time goes in v1:
time: 386 us
  waiting for transfers between devices  299 us (77%)
  matrix products  45.3 us (12%)
  other arithmetic  15 us (4%)
  between operations  13.3 us (3%)
  local copies, waits for them, and re-layouts  12.6 us (3%)
    all_gather x3, waiting for transfers between devices, gather_weight(): whole = lax.all_gather(own, ('grp', 'seq', 'sub'), axis=0, tiled=True)  253 us
    reduce_scatter x1, waiting for transfers between devices, body(): lax.psum_scatter(partial_sum.astype(jnp.bfloat16), 'head', scatter_dimens...  27.3 us
    all_gather x1, waiting for transfers between devices, body(): piece = lax.all_gather(stacked, ('seq', 'sub'), axis=0, tiled=True)  18.8 us
    dot_general x2, matrix products, visit(): jnp.einsum('grqk,kgd->grqd', probs, values_here, preferred_element_type=j...  10.3 us
    reduce_sum x2, other arithmetic, visit(): weight_sum = weight_sum * scaling + jnp.sum(weights, axis=3)  9.65 us
    dot_general x2, matrix products, visit(): jnp.einsum('qgrd,kgd->grqk', grouped, keys_here, preferred_element_type=j...  9.61 us
    dot_general x2, matrix products, project(): first = jnp.dot(normed, both[0], preferred_element_type=jnp.float32)  9.26 us
  transfers between devices with their start and end apart: 5, of which 5 were waited for; matrix products, arithmetic and copies ran while one was open for 14% of the time, Pallas kernels for 0%

profile of v1, /device:TPU:0, one launch (start us, length us, event | category | flops | bytes accessed | tf_op | source)
XLA Modules:
  0.0 385.7 jit_solution(14634166440619442348)
XLA Ops:
  6.6 1.3 constant_dynamic-slice_fusion.2
  7.9 0.8 fusion.30
  8.8 1.0 constant_dynamic-slice_fusion.1
  9.8 0.0 all-gather.8.cloned.1.call-start
  9.9 0.1 broadcast_compare_fusion.1
  10.0 0.1 slice_reduce_fusion.1
  10.1 1.9 fusion.21
  12.0 68.7 %all-gather.10.cloned.1.call-done = bf16[1,7168,512]{2,1,0:T(8,128)(2,1)} async-done(((bf16[1,448,512]{2,1,0:T(8,128)(2,1)}), bf16[1,7168,512]{2,1,0:T(8,128)(2,1)}) %all-gather.10.cloned.1.call-update) | async-done | bytes 7340048 | tf_op jit(solution)/shard_map/all_gather | solution.py:26
  80.7 3.9 %fusion.24 = bf16[256,512]{1,0:T(8,128)(2,1)S(1)} fusion(bf16[1,7168,512]{2,1,0:T(8,128)(2,1)} %all-gather.10.cloned.1.call-done, bf16[256,3584]{1,0:T(8,128)(2,1)} %param.10, f32[3584]{0:T(1024)S(1)} %get-tuple-element.274, f32[3584]{0:T(1024)S(1)} %get-tuple-element.273, f32[256]{0:T(256)S(1)} %add_rsqrt_fusion, pred[256]{0:T(512)(128)(4,1)S(1)} %get-tuple-element.301), kind=kOutput, calls=%fused_computation.38 | convolution fusion | flops 944111616 | bytes 5797120 | tf_op jit(solution)/shard_map/dot_general | solution.py:54
  84.6 1.4 copy-done.7
  86.0 1.9 fusion.29
  88.0 2.3 dynamic-slice_bitcast_fusion
  90.4 0.1 dynamic_slice.48
  90.4 0.1 fusion.31
  90.5 0.1 convert_bitcast_fusion
  90.6 0.3 reduce-window.9
  90.9 0.1 slice.85
  91.0 0.1 slice_reduce_fusion.2
  91.1 0.1 add_bitcast_fusion
  91.2 0.1 dynamic_slice.49
  91.2 104.1 %all-gather.12.cloned.1.call-done = bf16[1,7168,1024]{2,1,0:T(8,128)(2,1)} async-done(((bf16[1,448,1024]{2,1,0:T(8,128)(2,1)}), bf16[1,7168,1024]{2,1,0:T(8,128)(2,1)}) %all-gather.12.cloned.1.call-update) | async-done | bytes 14680080 | tf_op jit(solution)/shard_map/all_gather | solution.py:26
  195.4 5.4 %fusion.17 = bf16[256,1024]{1,0:T(8,128)(2,1)S(1)} fusion(bf16[1,7168,1024]{2,1,0:T(8,128)(2,1)} %all-gather.12.cloned.1.call-done, bf16[256,3584]{1,0:T(8,128)(2,1)S(1)} %copy-done.2, f32[3584]{0:T(1024)S(1)} %get-tuple-element.274, f32[3584]{0:T(1024)S(1)} %get-tuple-element.273, f32[256]{0:T(256)S(1)} %add_rsqrt_fusion, ...), kind=kOutput, calls=%fused_computation.27 | convolution fusion | flops 1883635712 | bytes 9729280 | tf_op jit(solution)/shard_map/dot_general | solution.py:54
  200.7 2.0 copy-done.6
  202.7 2.2 fusion.27
  205.0 0.4 reshape.79
  205.4 0.1 copy.15
  205.4 18.8 %all-gather.8.cloned.1.call-done = bf16[2048,512]{1,0:T(8,128)(2,1)} async-done(((bf16[256,512]{1,0:T(8,128)(2,1)}), bf16[2048,512]{1,0:T(8,128)(2,1)}) %all-gather.8.cloned.1.call-update) | async-done | bytes 2097168 | tf_op jit(solution)/shard_map/all_gather | solution.py:98
  224.2 35.0 %while.18 = (s32[]{:T(128)}, f32[2,4,256]{2,1,0:T(4,128)S(1)}, f32[2,4,256]{2,1,0:T(4,128)S(1)}, f32[2,4,256,128]{3,2,1,0:T(8,128)S(1)}, s32[256]{0:T(256)S(1)},...) while((s32[]{:T(128)}, f32[2,4,256]{2,1,0:T(4,128)S(1)}, ...), condition=%wide.region_6.7_spmd.clone, body=%wide.region_3.6_spmd.clone.sunk | while | flops 1103375872 | bytes 34248440 | solution.py:107
  224.3 0.9 or_and_fusion.2
  225.2 1.3 fusion.55
  226.5 0.2 copy.29
  226.7 4.8 %fusion.56 = (f32[2,4,256]{2,1,0:T(4,128)S(1)}, f32[2,1024,256,4]{2,1,3,0:T(8,128)}) fusion(pred[256,1024]{0,1:T(8,128)(4,1)S(1)} %or_and_fusion.2, bf16[1024,2,128,1]{0,2,3,1:T(8,128)(2,1)S(1)} %bitcast.83, bf16[256,2,4,128]{3,0,2,1:T(8,128)(2,1)S(1)} %get-tuple-element.438), kind=kOutput, calls=%fused_computation.3.clone.1 | convolution fusion | flops 543160320 | bytes 9707520 | tf_op jit(solution)/shard_map/while/body/eval_jaxpr/qgrd,kgd->grqk/dot_general | solution.py:79
  231.5 5.1 %fusion.57 = f32[2,4,256]{2,1,0:T(4,128)S(1)} fusion(f32[2,1024,256,4]{2,1,3,0:T(8,128)} %get-tuple-element.390, f32[2,4,256]{2,1,0:T(4,128)S(1)} %select_maximum_fusion.2, pred[256,1024]{0,1:T(8,128)(4,1)S(1)} %or_and_fusion.2), kind=kLoop, calls=%fused_computation.5.clone.1 | loop fusion | flops 10483712 | bytes 8667136 | tf_op jit(solution)/shard_map/while/body/eval_jaxpr/reduce_sum | solution.py:86
  236.7 0.2 copy.30
  236.9 5.1 %fusion.59 = f32[2,4,256,128]{3,2,1,0:T(8,128)S(1)} fusion(bf16[1024,2,128,1]{0,2,3,1:T(8,128)(2,1)S(1)} %bitcast.84, f32[2,1024,256,4]{2,1,3,0:T(8,128)} %get-tuple-element.390, f32[2,4,256]{2,1,0:T(4,128)S(1)} %select_maximum_fusion.2, pred[256,1024]{0,1:T(8,128)(4,1)S(1)} %or_and_fusion.2, f32[2,4,256,128]{3,2,1,0:T(8,128)S(1)} %get-tuple-element.414, ...), kind=kOutput, calls=%fused_computation.8.clone.1 | convolution fusion | flops 548143104 | bytes 11288577 | tf_op jit(solution)/shard_map/while/body/eval_jaxpr/grqk,kgd->grqd/dot_general | solution.py:88
  242.1 0.9 or_and_fusion.2
  243.0 1.3 fusion.55
  244.3 0.2 copy.29
  244.5 4.8 %fusion.56 = (f32[2,4,256]{2,1,0:T(4,128)S(1)}, f32[2,1024,256,4]{2,1,3,0:T(8,128)}) fusion(pred[256,1024]{0,1:T(8,128)(4,1)S(1)} %or_and_fusion.2, bf16[1024,2,128,1]{0,2,3,1:T(8,128)(2,1)S(1)} %bitcast.83, bf16[256,2,4,128]{3,0,2,1:T(8,128)(2,1)S(1)} %get-tuple-element.438), kind=kOutput, calls=%fused_computation.3.clone.1 | convolution fusion | flops 543160320 | bytes 9707520 | tf_op jit(solution)/shard_map/while/body/eval_jaxpr/qgrd,kgd->grqk/dot_general | solution.py:79
  249.3 4.5 %fusion.57 = f32[2,4,256]{2,1,0:T(4,128)S(1)} fusion(f32[2,1024,256,4]{2,1,3,0:T(8,128)} %get-tuple-element.390, f32[2,4,256]{2,1,0:T(4,128)S(1)} %select_maximum_fusion.2, pred[256,1024]{0,1:T(8,128)(4,1)S(1)} %or_and_fusion.2), kind=kLoop, calls=%fused_computation.5.clone.1 | loop fusion | flops 10483712 | bytes 8667136 | tf_op jit(solution)/shard_map/while/body/eval_jaxpr/reduce_sum | solution.py:86
  253.9 0.2 copy.30
  254.1 5.2 %fusion.59 = f32[2,4,256,128]{3,2,1,0:T(8,128)S(1)} fusion(bf16[1024,2,128,1]{0,2,3,1:T(8,128)(2,1)S(1)} %bitcast.84, f32[2,1024,256,4]{2,1,3,0:T(8,128)} %get-tuple-element.390, f32[2,4,256]{2,1,0:T(4,128)S(1)} %select_maximum_fusion.2, pred[256,1024]{0,1:T(8,128)(4,1)S(1)} %or_and_fusion.2, f32[2,4,256,128]{3,2,1,0:T(8,128)S(1)} %get-tuple-element.414, ...), kind=kOutput, calls=%fused_computation.8.clone.1 | convolution fusion | flops 548143104 | bytes 11288577 | tf_op jit(solution)/shard_map/while/body/eval_jaxpr/grqk,kgd->grqd/dot_general | solution.py:88
  259.3 0.3 copy.16
  259.6 0.1 divide_convert_fusion
  259.7 80.1 %all-gather.14.cloned.1.call-done = bf16[1,7168,1024]{2,1,0:T(8,128)(2,1)} async-done(((bf16[1,448,1024]{2,1,0:T(8,128)(2,1)}), bf16[1,7168,1024]{2,1,0:T(8,128)(2,1)}) %all-gather.14.cloned.1.call-update) | async-done | bytes 14680080 | tf_op jit(solution)/shard_map/all_gather | solution.py:26
  339.9 5.2 %fusion.15 = bf16[256,3584]{1,0:T(8,128)(2,1)S(1)} fusion(bf16[256,1024]{0,1:T(8,128)(2,1)S(1)} %bitcast.85, bf16[1,7168,1024]{2,1,0:T(8,128)(2,1)} %all-gather.14.cloned.1.call-done), kind=kOutput, calls=%fused_computation.23 | convolution fusion | flops 1879048192 | bytes 9699328 | tf_op jit(solution)/shard_map/dot_general | solution.py:115
  345.1 6.8 %fusion.20 = bf16[256,3584]{1,0:T(8,128)(2,1)} fusion(bf16[256,3584]{1,0:T(8,128)(2,1)S(1)} %fusion.15, bf16[256,1024]{0,1:T(8,128)(2,1)S(1)} %bitcast.86, bf16[1,7168,1024]{2,1,0:T(8,128)(2,1)} %all-gather.14.cloned.1.call-done, pred[256]{0:T(512)(128)(4,1)S(1)} %get-tuple-element.301), kind=kOutput, calls=%fused_computation.31 | convolution fusion | flops 1879965696 | bytes 11534592 | tf_op jit(solution)/shard_map/dot_general | solution.py:116
  351.9 27.3 %reduce-scatter.2.cloned.1.call-done = bf16[256,1792]{1,0:T(8,128)(2,1)} async-done(((bf16[256,3584]{1,0:T(8,128)(2,1)}), bf16[256,1792]{1,0:T(8,128)(2,1)}) %reduce-scatter.2.cloned.1.call-update) | async-done | bytes 917520 | tf_op jit(solution)/shard_map/reduce_scatter | solution.py:118
  (44 shorter events, 0.4 us)
Async XLA Ops:
  6.5 2.3 copy-start
  6.5 3.3 copy-start.4
  6.5 3.4 copy-start.5
  6.5 74.2 %all-gather.10.cloned.1.call-start = ((), (), s32[]{:S(2)}) async-start(), calls=%async_computation.3 | async-start | bytes 7798784 | tf_op jit(solution)/shard_map/all_gather | solution.py:26
  8.8 186.6 %all-gather.12.cloned.1.call-start = ((), (), s32[]{:S(2)}) async-start(), calls=%async_computation.4 | async-start | bytes 15597568 | tf_op jit(solution)/shard_map/all_gather | solution.py:26
  9.8 214.4 %all-gather.8.cloned.1.call-start = ((), (), s32[]{:S(2)}) async-start(), calls=%async_computation.1 | async-start | bytes 2359296 | tf_op jit(solution)/shard_map/all_gather | solution.py:98
  80.7 3.9 %copy-start.2 = (bf16[256,3584]{1,0:T(8,128)(2,1)S(1)}, bf16[256,3584]{1,0:T(8,128)(2,1)}, u32[]{:S(2)}) copy-start(bf16[256,3584]{1,0:T(8,128)(2,1)} %param.10) | copy-start | bytes 5505028
  80.7 5.3 %copy-start.7 = (bf16[1,7168,512]{2,1,0:T(8,128)(2,1)S(1)}, bf16[1,7168,512]{2,1,0:T(8,128)(2,1)}, u32[]{:S(2)}) copy-start(bf16[1,7168,512]{2,1,0:T(8,128)(2,1)} %all-gather.10.cloned.1.call-done) | copy-start | bytes 22020100
  86.0 4.4 %copy-start.3 = (s32[2048]{0:T(1024)S(1)}, s32[2048]{0:T(1024)}, u32[]{:S(2)}) copy-start(s32[2048]{0:T(1024)} %param.17) | copy-start | bytes 24580
  87.9 251.9 %all-gather.14.cloned.1.call-start = ((), (), s32[]{:S(2)}) async-start(), calls=%async_computation.5 | async-start | bytes 15597568 | tf_op jit(solution)/shard_map/all_gather | solution.py:26
  90.3 288.9 %reduce-scatter.2.cloned.1.call-start = ((), (), s32[]{:S(2)}) async-start(), calls=%async_computation.2 | async-start | bytes 2752512 | tf_op jit(solution)/shard_map/reduce_scatter | solution.py:118
  195.3 7.4 %copy-start.6 = (bf16[1,7168,1024]{2,1,0:T(8,128)(2,1)S(1)}, bf16[1,7168,1024]{2,1,0:T(8,128)(2,1)}, u32[]{:S(2)}) copy-start(bf16[1,7168,1024]{2,1,0:T(8,128)(2,1)} %all-gather.12.cloned.1.call-done) | copy-start | bytes 44040196
  345.1 34.1 %copy-start.1 = (bf16[2,448,1024]{2,1,0:T(8,128)(2,1)S(1)}, bf16[2,448,1024]{2,1,0:T(8,128)(2,1)}, u32[]{:S(2)}) copy-start(bf16[2,448,1024]{2,1,0:T(8,128)(2,1)} %param.12) | copy-start | bytes 5505028
Sparse Core Ops, SparseCore 0:
  9.7 70.9 all-gather.9
  83.0 112.2 all-gather.11
  197.0 27.2 all-gather.7
  226.4 113.3 all-gather.13
  352.0 27.0 reduce-scatter.1

commit v2 on v1

--- a/solution.py
+++ b/solution.py
@@ -1,10 +1,14 @@
+import functools
 import math
 
 import jax
 import jax.numpy as jnp
 from jax import lax
+from jax.experimental import pallas as pl
+from jax.experimental.pallas import tpu as pltpu
 from jax.sharding import PartitionSpec as P
 
+MESH = pl.DeviceIdType.MESH
 HEAD_DIM = 128
 KV_HEADS = 4
 
@@ -18,19 +22,146 @@
     return jnp.cumsum(begins)
 
 
-def gather_weight(shard):
-    both, _, columns = shard.shape
-    if lax.axis_size("grp") != both:
-        return lax.all_gather(shard, ("seq", "sub"), axis=1, tiled=True)
-    own = lax.dynamic_index_in_dim(shard, lax.axis_index("grp"), 0, keepdims=False)
-    whole = lax.all_gather(own, ("grp", "seq", "sub"), axis=0, tiled=True)
-    return whole.reshape(both, -1, columns)
+def cut(rows):
+    count = next(c for c in (4, 2, 1) if rows % (16 * c) == 0 or c == 1)
+    return [(i * (rows // count), rows // count) for i in range(count)]
+
+
+def gather_kernel(count, pieces, firsts, *refs):
+    sources, wholes = refs[:count], refs[count : 2 * count]
+    seq_recv, grp_recv, sub_recv, up_send, down_send, grp_send, sub_send, local = refs[2 * count :]
+    n = lax.axis_size("seq")
+    plane, z, core = lax.axis_index("grp"), lax.axis_index("seq"), lax.axis_index("sub")
+    up, down = {"seq": z + 1}, {"seq": z - 1}
+    across, beside = {"grp": 1 - plane}, {"sub": 1 - core}
+    has_up, has_down = z < n - 1, z > 0
+
+    barrier = pltpu.get_barrier_semaphore()
+
+    def greet(device):
+        pl.semaphore_signal(barrier, inc=1, device_id=device, device_id_type=MESH)
+
+    greet(across)
+    greet(beside)
+    pl.when(has_up)(lambda: greet(up))
+    pl.when(has_down)(lambda: greet(down))
+    pl.semaphore_wait(barrier, 2 + has_up.astype(jnp.int32) + has_down.astype(jnp.int32))
+
+    def own(mod, k):
+        which, offset, height = pieces[k]
+        columns = wholes[which].shape[2]
+        return sources[which].at[mod, pl.ds(offset, height), pl.ds(firsts(which), columns)]
+
+    def place(mod, s, c, k):
+        which, offset, height = pieces[k]
+        shard = sources[which].shape[1]
+        start = pl.multiple_of((s * 2 + c) * shard + offset, 16)
+        return wholes[which].at[mod, pl.ds(start, height)]
+
+    def remote(src, mod, s, k, send, recv, device):
+        return pltpu.make_async_remote_copy(
+            src_ref=src,
+            dst_ref=place(mod, s, core, k),
+            send_sem=send,
+            recv_sem=recv,
+            device_id=device,
+            device_id_type=MESH,
+        )
+
+    def to_up(src, s, k):
+        return remote(src, plane, s, k, up_send.at[s, k], seq_recv.at[s, k], up)
+
+    def to_down(src, s, k):
+        return remote(src, plane, s, k, down_send.at[s, k], seq_recv.at[s, k], down)
+
+    def to_across(src, s, k):
+        return remote(src, plane, s, k, grp_send.at[s, k], grp_recv.at[s, k], across)
+
+    def to_beside(src, mod, s, k):
+        return remote(src, mod, s, k, sub_send.at[mod, s, k], sub_recv.at[mod, s, k], beside)
+
+    every = range(len(pieces))
+    for k in every:
+        pl.when(has_up)(lambda: to_up(own(plane, k), z, k).start())
+        pl.when(has_down)(lambda: to_down(own(plane, k), z, k).start())
+    for k in every:
+        for mod in range(2):
+            to_beside(own(mod, k), mod, z, k).start()
+            pltpu.make_async_copy(own(mod, k), place(mod, z, core, k), local.at[mod, k]).start()
+
+    def arrived(s, k, onward, further):
+        here = place(plane, s, core, k)
+        onward(here, s, k).wait_recv()
+        pl.when(further)(lambda: onward(here, s, k).start())
+        to_across(here, s, k).start()
+        to_beside(here, plane, s, k).start()
+
+    def crossed(s, k):
+        here = place(1 - plane, s, core, k)
+        remote(here, 1 - plane, s, k, grp_send.at[s, k], grp_recv.at[s, k], across).wait_recv()
+        to_beside(here, 1 - plane, s, k).start()
+
+    steps = [(d, k) for d in range(1, n) for k in every]
+    for number in range(len(steps) + 1):
+        if number < len(steps):
+            d, k = steps[number]
+            pl.when(z >= d)(lambda: arrived(z - d, k, to_up, has_up))
+            pl.when(z + d < n)(lambda: arrived(z + d, k, to_down, has_down))
+        if number > 0:
+            d, k = steps[number - 1]
+            pl.when(z >= d)(lambda: crossed(z - d, k))
+            pl.when(z + d < n)(lambda: crossed(z + d, k))
+
+    for s in range(n):
+        for k in every:
+            here = place(plane, s, core, k)
+
+            def sent_on(s=s, k=k, here=here):
+                to_across(here, s, k).wait_send()
+
+            pl.when(z != s)(sent_on)
+            pl.when(has_up & (s <= z))(lambda: to_up(here, s, k).wait_send())
+            pl.when(has_down & (s >= z))(lambda: to_down(here, s, k).wait_send())
+            for mod in range(2):
+                copy = to_beside(place(mod, s, core, k), mod, s, k)
+                copy.wait_send()
+                copy.wait_recv()
+    for k in every:
+        for mod in range(2):
+            pltpu.make_async_copy(own(mod, k), place(mod, z, core, k), local.at[mod, k]).wait()
+
+
+def gather_weights(shards, widths, firsts, collective_id):
+    n = lax.axis_size("seq")
+    if lax.axis_size("grp") != 2 or lax.axis_size("sub") != 2:
+        return [
+            lax.all_gather(
+                lax.dynamic_slice_in_dim(x, firsts(i), widths[i], 2), ("seq", "sub"), axis=1, tiled=True
+            )
+            for i, x in enumerate(shards)
+        ]
+    pieces = [(i, *piece) for i, x in enumerate(shards) for piece in cut(x.shape[1])]
+    total = len(pieces)
+    shapes = [
+        jax.ShapeDtypeStruct((2, 2 * n * x.shape[1], width), x.dtype)
+        for x, width in zip(shards, widths)
+    ]
+    moved = sum(2 * math.prod(shape.shape) for shape in shapes)
+    semaphores = [(n, total), (n, total), (2, n, total)] + [(n, total)] * 3 + [(2, n, total), (2, total)]
+    return pl.pallas_call(
+        functools.partial(gather_kernel, len(shards), pieces, firsts),
+        out_shape=shapes,
+        in_specs=[pl.BlockSpec(memory_space=pl.ANY)] * len(shards),
+        out_specs=[pl.BlockSpec(memory_space=pl.ANY)] * len(shards),
+        scratch_shapes=[pltpu.SemaphoreType.DMA(shape) for shape in semaphores],
+        compiler_params=pltpu.CompilerParams(collective_id=collective_id, has_side_effects=True),
+        cost_estimate=pl.CostEstimate(flops=0, bytes_accessed=8 * moved, transcendentals=0),
+    )(*shards)
 
 
 def body(tokens, norm_gain, w_query, w_key, w_value, w_out, modality, doc_ids):
     length = tokens.shape[0]
     head_count = lax.axis_size("head")
-    head_index = lax.axis_index("head")
     first_pos = lax.axis_index(("seq", "sub")) * length
     blocks = block_ids(modality, doc_ids)
     own_mod = lax.dynamic_slice_in_dim(modality, first_pos, length)
@@ -38,24 +169,32 @@
     own_block = lax.dynamic_slice_in_dim(blocks, first_pos, length)
     generate = (own_mod == 1)[:, None]
     kv_local = max(KV_HEADS // head_count, 1)
-    kv_first = head_index * KV_HEADS // head_count
-    key_cols = lax.dynamic_slice_in_dim(w_key, kv_first * HEAD_DIM, kv_local * HEAD_DIM, 2)
-    value_cols = lax.dynamic_slice_in_dim(w_value, kv_first * HEAD_DIM, kv_local * HEAD_DIM, 2)
     values32 = tokens.astype(jnp.float32)
     factor = lax.rsqrt(jnp.mean(values32 * values32, axis=1, keepdims=True) + EPS)
     gain = jnp.where(generate, norm_gain[1][None, :], norm_gain[0][None, :])
     normed = (values32 * factor * gain).astype(jnp.bfloat16)
-    key_value_weight = jnp.concatenate([key_cols, value_cols], axis=2)
-    kv_both = gather_weight(key_value_weight)
-    q_both = gather_weight(w_query)
-    out_both = gather_weight(jnp.swapaxes(w_out, 1, 2))
+    kv_width = kv_local * HEAD_DIM
+
+    def first_column(which):
+        if which == 2:
+            return 0
+        return pl.multiple_of(lax.axis_index("head") * KV_HEADS // head_count * HEAD_DIM, HEAD_DIM)
+
+    key_both, value_both, q_both = gather_weights(
+        [w_key, w_value, w_query], [kv_width, kv_width, w_query.shape[2]], first_column, 0
+    )
+    w_out = jnp.swapaxes(w_out, 1, 2)
+    w_out, key_both, value_both, q_both = lax.optimization_barrier(
+        (w_out, key_both, value_both, q_both)
+    )
+    (out_both,) = gather_weights([w_out], [w_out.shape[2]], lambda which: 0, 1)
 
     def project(both):
         first = jnp.dot(normed, both[0], preferred_element_type=jnp.float32)
         second = jnp.dot(normed, both[1], preferred_element_type=jnp.float32)
         return jnp.where(generate, second, first).astype(jnp.bfloat16)
 
-    stacked = project(kv_both)
+    stacked = jnp.concatenate([project(key_both), project(value_both)], axis=1)
     query = project(q_both)
     q_local = query.shape[1] // HEAD_DIM
     repeat = q_local // kv_local

time: 386 us -> 306 us (0.79)
  waiting for transfers between devices: 299 us -> 28.3 us
  Pallas kernels: 0 us -> 199 us
  local copies, waits for them, and re-layouts: 12.6 us -> 7.01 us
    all_gather x3 -> x0, waiting for transfers between devices: 253 us -> none  [gather_weight(): whole = lax.all_gather(own, ('grp', 'seq', 'sub'), axis=0, tiled=True)]
    pallas_call x0 -> x2, Pallas kernels: none -> 199 us  [gather_weights(): pl.pallas_call(functools.partial(gather_kernel, len(shards), pieces, firs...]
    all_gather x1, waiting for transfers between devices: 18.8 us -> 0.02 us  [body(): piece = lax.all_gather(stacked, ('seq', 'sub'), axis=0, tiled=True)]
    dynamic_slice x3 -> x0, local copies, waits for them, and re-layouts: 4.6 us -> none  [the longest x2 3.25 us: gather_weight(): lax.dynamic_index_in_dim(shard, lax.axis_index('grp'), 0, keepdims=False)]
    dot_general x2, matrix products: 10.3 us -> 6.07 us  [visit(): jnp.einsum('grqk,kgd->grqd', probs, values_here, preferred_element_type=j...]
    dot_general x2 -> x3, matrix products: 4.16 us -> 7.94 us  [project(): second = jnp.dot(normed, both[1], preferred_element_type=jnp.float32)]
    dot_general x2 -> x3, matrix products: 9.26 us -> 9.21 us  [project(): first = jnp.dot(normed, both[0], preferred_element_type=jnp.float32)]
  transfers between devices with their start and end apart: 5 -> 2, of which waited for: 5 -> 1; matrix products, arithmetic and copies ran while one was open for 14% -> 4% of each run, Pallas kernels for 0% -> 28%
where the time goes in v2:
time: 306 us
  Pallas kernels  199 us (65%)
  matrix products  44.7 us (15%)
  waiting for transfers between devices  28.3 us (9%)
  between operations  13.6 us (4%)
  other arithmetic  13 us (4%)
  local copies, waits for them, and re-layouts  7.01 us (2%)
    pallas_call x2, Pallas kernels, gather_weights(): pl.pallas_call(functools.partial(gather_kernel, len(shards), pieces, firs...  199 us
    reduce_scatter x1, waiting for transfers between devices, body(): lax.psum_scatter(partial_sum.astype(jnp.bfloat16), 'head', scatter_dimens...  28.2 us
    dot_general x2, matrix products, visit(): jnp.einsum('qgrd,kgd->grqk', grouped, keys_here, preferred_element_type=j...  9.67 us
    dot_general x3, matrix products, project(): first = jnp.dot(normed, both[0], preferred_element_type=jnp.float32)  9.21 us
    reduce_sum x2, other arithmetic, visit(): weight_sum = weight_sum * scaling + jnp.sum(weights, axis=3)  9.21 us
    dot_general x3, matrix products, project(): second = jnp.dot(normed, both[1], preferred_element_type=jnp.float32)  7.94 us
    dot_general x1, matrix products, body(): lax.dot_general(attended, out_both[1], contract, preferred_element_type=j...  6.65 us
  transfers between devices with their start and end apart: 2, of which 1 were waited for; matrix products, arithmetic and copies ran while one was open for 4% of the time, Pallas kernels for 28%

profile of v2, /device:TPU:0, one launch (start us, length us, event | category | flops | bytes accessed | tf_op | source)
XLA Modules:
  0.0 305.7 jit_solution(15414666074032204518)
XLA Ops:
  6.5 0.0 all-gather.2.cloned.1.call-start
  6.5 114.2 %shard_map.82 = (bf16[2,3584,256]{2,1,0:T(8,128)(2,1)}, bf16[2,3584,256]{2,1,0:T(8,128)(2,1)}, bf16[2,3584,1024]{2,1,0:T(8,128)(2,1)}) custom-call(bf16[2,448,512]{2,1,0:T(8,128)(2,1)} %refs_0_.1, bf16[2,448,512]{2,1,0:T(8,128)(2,1)} %refs_1_.1, bf16[2,448,1024]{2,1,0:T(8,128)(2,1)} %refs_2_.1), custom_call_target="tpu_custom_call" | custom-call | bytes 176160768 | tf_op jit(solution)/shard_map/pallas_call | solution.py:151
  120.7 0.0 copy-done.4
  120.7 0.1 slice_reduce_fusion.1
  120.8 0.4 fusion.33
  121.3 0.1 broadcast_compare_fusion.1
  121.4 2.8 fusion.40
  124.2 1.2 fusion.63
  125.4 0.8 copy-done.5
  126.2 1.2 fusion.36
  127.4 1.2 fusion.60
  128.7 0.7 pad_maximum_fusion
  129.4 0.0 all-gather.2.cloned.1.call-update
  129.4 0.2 reduce-scatter.2.cloned.1.call-start
  129.7 5.2 %fusion.19 = bf16[256,1024]{1,0:T(8,128)(2,1)S(1)} fusion(bf16[2,3584,1024]{2,1,0:T(8,128)(2,1)} %get-tuple-element.217, bf16[256,3584]{1,0:T(8,128)(2,1)S(1)} %copy-done.1, f32[3584]{0:T(1024)S(1)} %get-tuple-element.288, f32[3584]{0:T(1024)S(1)} %get-tuple-element.287, f32[256]{0:T(256)S(1)} %add_rsqrt_fusion, pred[256]{0:T(512)(128)(4,1)S(1)} %get-tuple-element.315), kind=kOutput, calls=%fused_computation.26 | convolution fusion | flops 1883635712 | bytes 9729280 | tf_op jit(solution)/shard_map/dot_general | solution.py:193
  134.9 0.0 copy-start.2
  134.9 5.5 %fusion.51 = bf16[256,1024]{1,0:T(8,128)(2,1)S(1)} fusion(bf16[256,1024]{1,0:T(8,128)(2,1)S(1)} %fusion.19, bf16[2,3584,1024]{2,1,0:T(8,128)(2,1)} %get-tuple-element.217, pred[256]{0:T(512)(128)(4,1)S(1)} %get-tuple-element.315, bf16[256,3584]{1,0:T(8,128)(2,1)S(1)} %copy-done.1, f32[3584]{0:T(1024)S(1)} %get-tuple-element.288, ...), kind=kOutput, calls=%fused_computation.54 | convolution fusion | flops 1883897856 | bytes 10258432 | tf_op jit(solution)/shard_map/dot_general | solution.py:194
  140.4 0.4 reshape.64
  140.8 0.1 copy.15
  140.9 0.1 dynamic_slice.31
  140.9 0.1 fusion.66
  141.0 0.1 convert_bitcast_fusion
  141.1 0.3 reduce-window.9
  141.4 0.1 slice.81
  141.5 0.1 slice_reduce_fusion.2
  141.6 0.1 add_bitcast_fusion
  141.7 0.1 dynamic_slice.32
  141.8 84.5 %shard_map.83 = bf16[2,3584,1024]{2,1,0:T(8,128)(2,1)} custom-call(bf16[2,448,1024]{2,1,0:T(8,128)(2,1)} %bitcast.94), custom_call_target="tpu_custom_call" | custom-call | bytes 117440512 | tf_op jit(solution)/shard_map/pallas_call | solution.py:151
  226.3 0.0 all-gather.2.cloned.1.call-done
  226.3 32.0 %while.18 = (s32[]{:T(128)}, f32[2,4,256]{2,1,0:T(4,128)S(1)}, f32[2,4,256]{2,1,0:T(4,128)S(1)}, f32[2,4,256,128]{3,2,1,0:T(8,128)S(1)}, s32[256]{0:T(256)S(1)},...) while((s32[]{:T(128)}, f32[2,4,256]{2,1,0:T(4,128)S(1)}, ...), condition=%wide.region_6.7_spmd.clone, body=%wide.region_3.6_spmd.clone.sunk | while | flops 1103375872 | bytes 65705748 | solution.py:246
  226.4 0.9 or_and_fusion.2
  227.3 1.3 fusion.92
  228.6 4.8 %fusion.93 = (f32[2,4,256]{2,1,0:T(4,128)S(1)}, f32[2,1024,256,4]{2,1,3,0:T(8,128)}) fusion(pred[256,1024]{0,1:T(8,128)(4,1)S(1)} %or_and_fusion.2, bf16[1024,2,128,1]{0,2,3,1:T(8,128)(2,1)S(1)} %bitcast.92, bf16[256,2,4,128]{3,0,2,1:T(8,128)(2,1)S(1)} %get-tuple-element.450), kind=kOutput, calls=%fused_computation.3.clone.1 | convolution fusion | flops 543160320 | bytes 9707520 | tf_op jit(solution)/shard_map/while/body/eval_jaxpr/qgrd,kgd->grqk/dot_general | solution.py:218
  233.5 4.6 %fusion.94 = f32[2,4,256]{2,1,0:T(4,128)S(1)} fusion(f32[2,1024,256,4]{2,1,3,0:T(8,128)} %get-tuple-element.402, f32[2,4,256]{2,1,0:T(4,128)S(1)} %select_maximum_fusion.2, pred[256,1024]{0,1:T(8,128)(4,1)S(1)} %or_and_fusion.2), kind=kLoop, calls=%fused_computation.5.clone.1 | loop fusion | flops 10483712 | bytes 8667136 | tf_op jit(solution)/shard_map/while/body/eval_jaxpr/reduce_sum | solution.py:225
  238.1 1.2 copy-done
  239.3 3.0 fusion.96
  242.4 0.9 or_and_fusion.2
  243.3 1.3 fusion.92
  244.6 4.8 %fusion.93 = (f32[2,4,256]{2,1,0:T(4,128)S(1)}, f32[2,1024,256,4]{2,1,3,0:T(8,128)}) fusion(pred[256,1024]{0,1:T(8,128)(4,1)S(1)} %or_and_fusion.2, bf16[1024,2,128,1]{0,2,3,1:T(8,128)(2,1)S(1)} %bitcast.92, bf16[256,2,4,128]{3,0,2,1:T(8,128)(2,1)S(1)} %get-tuple-element.450), kind=kOutput, calls=%fused_computation.3.clone.1 | convolution fusion | flops 543160320 | bytes 9707520 | tf_op jit(solution)/shard_map/while/body/eval_jaxpr/qgrd,kgd->grqk/dot_general | solution.py:218
  249.5 4.6 %fusion.94 = f32[2,4,256]{2,1,0:T(4,128)S(1)} fusion(f32[2,1024,256,4]{2,1,3,0:T(8,128)} %get-tuple-element.402, f32[2,4,256]{2,1,0:T(4,128)S(1)} %select_maximum_fusion.2, pred[256,1024]{0,1:T(8,128)(4,1)S(1)} %or_and_fusion.2), kind=kLoop, calls=%fused_computation.5.clone.1 | loop fusion | flops 10483712 | bytes 8667136 | tf_op jit(solution)/shard_map/while/body/eval_jaxpr/reduce_sum | solution.py:225
  254.1 1.2 copy-done
  255.3 3.0 fusion.96
  258.4 0.3 copy.16
  258.7 0.1 divide_convert_fusion
  258.8 5.2 %fusion.15 = bf16[256,3584]{1,0:T(8,128)(2,1)S(1)} fusion(bf16[256,1024]{0,1:T(8,128)(2,1)S(1)} %bitcast.95, bf16[2,3584,1024]{2,1,0:T(8,128)(2,1)} %shard_map.83), kind=kOutput, calls=%fused_computation.22 | convolution fusion | flops 1879048192 | bytes 9699328 | tf_op jit(solution)/shard_map/dot_general | solution.py:254
  264.0 6.7 %fusion.30 = bf16[256,3584]{1,0:T(8,128)(2,1)} fusion(bf16[256,3584]{1,0:T(8,128)(2,1)S(1)} %fusion.15, bf16[256,1024]{0,1:T(8,128)(2,1)S(1)} %bitcast.96, bf16[2,3584,1024]{2,1,0:T(8,128)(2,1)} %shard_map.83, pred[256]{0:T(512)(128)(4,1)S(1)} %get-tuple-element.315), kind=kOutput, calls=%fused_computation.35 | convolution fusion | flops 1879965696 | bytes 11534592 | tf_op jit(solution)/shard_map/dot_general | solution.py:255
  270.7 0.0 reduce-scatter.2.cloned.1.call-update
  270.7 28.2 %reduce-scatter.2.cloned.1.call-done = bf16[256,1792]{1,0:T(8,128)(2,1)} async-done(((bf16[256,3584]{1,0:T(8,128)(2,1)}), bf16[256,1792]{1,0:T(8,128)(2,1)}) %reduce-scatter.2.cloned.1.call-update) | async-done | bytes 917520 | tf_op jit(solution)/shard_map/reduce_scatter | solution.py:257
  (32 shorter events, 0.2 us)
Async XLA Ops:
  6.5 114.2 %copy-start.4 = (f32[2,3584]{1,0:T(2,128)S(1)}, f32[2,3584]{1,0:T(2,128)}, u32[]{:S(2)}) copy-start(f32[2,3584]{1,0:T(2,128)} %param.11) | copy-start | bytes 86020
  6.5 114.3 %copy-start.1 = (bf16[256,3584]{1,0:T(8,128)(2,1)S(1)}, bf16[256,3584]{1,0:T(8,128)(2,1)}, u32[]{:S(2)}) copy-start(bf16[256,3584]{1,0:T(8,128)(2,1)} %param.10) | copy-start | bytes 5505028
  6.5 114.7 %copy-start.3 = (s32[2048]{0:T(1024)S(1)}, s32[2048]{0:T(1024)}, u32[]{:S(2)}) copy-start(s32[2048]{0:T(1024)} %param.16) | copy-start | bytes 24580
  6.5 219.8 %all-gather.2.cloned.1.call-start = ((), (), s32[]{:S(2)}) async-start(), calls=%async_computation.1 | async-start | bytes 2359296 | tf_op jit(solution)/shard_map/all_gather | solution.py:237
  121.4 2.8 copy-start.6
  124.2 2.0 copy-start.5
  129.4 169.5 %reduce-scatter.2.cloned.1.call-start = ((), (), s32[]{:S(2)}) async-start(), calls=%async_computation.2 | async-start | bytes 2752512 | tf_op jit(solution)/shard_map/reduce_scatter | solution.py:257
  134.9 6.0 %copy-start.2 = (s32[2048]{0:T(1024)S(1)}, s32[2048]{0:T(1024)}, u32[]{:S(2)}) copy-start(s32[2048]{0:T(1024)} %param.17) | copy-start | bytes 24580
  233.4 5.8 %copy-start = (f32[2,1024,256,4]{2,1,3,0:T(8,128)S(1)}, f32[2,1024,256,4]{2,1,3,0:T(8,128)}, u32[]{:S(2)}) copy-start(f32[2,1024,256,4]{2,1,3,0:T(8,128)} %get-tuple-element.402) | copy-start | bytes 25165828 | tf_op jit(solution)/shard_map/while
  249.5 5.8 %copy-start = (f32[2,1024,256,4]{2,1,3,0:T(8,128)S(1)}, f32[2,1024,256,4]{2,1,3,0:T(8,128)}, u32[]{:S(2)}) copy-start(f32[2,1024,256,4]{2,1,3,0:T(8,128)} %get-tuple-element.402) | copy-start | bytes 25165828 | tf_op jit(solution)/shard_map/while
Sparse Core Ops, SparseCore 0:
  129.5 41.5 all-gather.1
  270.8 28.0 reduce-scatter.1

commit v3 on v1

--- a/solution.py
+++ b/solution.py
@@ -1,10 +1,14 @@
+import functools
 import math
 
 import jax
 import jax.numpy as jnp
 from jax import lax
+from jax.experimental import pallas as pl
+from jax.experimental.pallas import tpu as pltpu
 from jax.sharding import PartitionSpec as P
 
+MESH = pl.DeviceIdType.MESH
 HEAD_DIM = 128
 KV_HEADS = 4
 
@@ -18,19 +22,350 @@
     return jnp.cumsum(begins)
 
 
-def gather_weight(shard):
-    both, _, columns = shard.shape
-    if lax.axis_size("grp") != both:
-        return lax.all_gather(shard, ("seq", "sub"), axis=1, tiled=True)
-    own = lax.dynamic_index_in_dim(shard, lax.axis_index("grp"), 0, keepdims=False)
-    whole = lax.all_gather(own, ("grp", "seq", "sub"), axis=0, tiled=True)
-    return whole.reshape(both, -1, columns)
+def cut(rows):
+    count = next(c for c in (4, 2, 1) if rows % (16 * c) == 0 or c == 1)
+    return [(i * (rows // count), rows // count) for i in range(count)]
+
+
+def greet(devices):
+    barrier = pltpu.get_barrier_semaphore()
+    present = jnp.int32(0)
+    for device, there in devices:
+
+        def signal(device=device):
+            pl.semaphore_signal(barrier, inc=1, device_id=device, device_id_type=MESH)
+
+        pl.when(there)(signal)
+        present = present + jnp.where(there, 1, 0)
+    pl.semaphore_wait(barrier, present)
+
+
+def neighbours():
+    n, z = lax.axis_size("seq"), lax.axis_index("seq")
+    return (
+        ({"seq": z + 1}, z < n - 1),
+        ({"seq": z - 1}, z > 0),
+        ({"grp": 1 - lax.axis_index("grp")}, z >= 0),
+        ({"sub": 1 - lax.axis_index("sub")}, z >= 0),
+    )
+
+
+def remote(src, dst, send, recv, device):
+    return pltpu.make_async_remote_copy(
+        src_ref=src, dst_ref=dst, send_sem=send, recv_sem=recv, device_id=device, device_id_type=MESH
+    )
+
+
+class Gather:
+    def __init__(self, pieces, firsts, sources, wholes, semaphores):
+        self.pieces, self.firsts, self.sources, self.wholes = pieces, firsts, sources, wholes
+        self.semaphores = semaphores
+        self.every = range(len(pieces))
+        self.n = lax.axis_size("seq")
+        self.steps = [(d, k) for d in range(1, self.n) for k in self.every]
+        self.plane, self.z, self.core = [lax.axis_index(axis) for axis in ("grp", "seq", "sub")]
+
+    def own(self, mod, k):
+        which, offset, height = self.pieces[k]
+        columns = self.wholes[which].shape[2]
+        return self.sources[which].at[
+            mod, pl.ds(offset, height), pl.ds(self.firsts(which), columns)
+        ]
+
+    def place(self, mod, s, c, k):
+        which, offset, height = self.pieces[k]
+        shard = self.sources[which].shape[1]
+        start = pl.multiple_of((s * 2 + c) * shard + offset, 16)
+        return self.wholes[which].at[mod, pl.ds(start, height)]
+
+    def along(self, src, s, k, way):
+        seq_recv, send = self.semaphores[0], self.semaphores[3 + way]
+        dst = self.place(self.plane, s, self.core, k)
+        return remote(src, dst, send.at[s, k], seq_recv.at[s, k], neighbours()[way][0])
+
+    def across(self, src, mod, s, k):
+        recv, send = self.semaphores[1], self.semaphores[5]
+        dst = self.place(mod, s, self.core, k)
+        return remote(src, dst, send.at[s, k], recv.at[s, k], neighbours()[2][0])
+
+    def beside(self, src, mod, s, k):
+        recv, send = self.semaphores[2], self.semaphores[6]
+        dst = self.place(mod, s, self.core, k)
+        return remote(src, dst, send.at[mod, s, k], recv.at[mod, s, k], neighbours()[3][0])
+
+    def local(self, mod, k):
+        dst = self.place(mod, self.z, self.core, k)
+        return pltpu.make_async_copy(self.own(mod, k), dst, self.semaphores[7].at[mod, k])
+
+    def start(self):
+        ways = neighbours()
+        for k in self.every:
+            for way in (0, 1):
+
+                def send(way=way, k=k):
+                    self.along(self.own(self.plane, k), self.z, k, way).start()
+
+                pl.when(ways[way][1])(send)
+        for k in self.every:
+            for mod in range(2):
+                self.beside(self.own(mod, k), mod, self.z, k).start()
+                self.local(mod, k).start()
+
+    def arrived(self, s, k, way):
+        here = self.place(self.plane, s, self.core, k)
+        self.along(here, s, k, way).wait_recv()
+        pl.when(neighbours()[way][1])(lambda: self.along(here, s, k, way).start())
+        self.across(here, self.plane, s, k).start()
+        self.beside(here, self.plane, s, k).start()
+
+    def crossed(self, s, k):
+        here = self.place(1 - self.plane, s, self.core, k)
+        self.across(here, 1 - self.plane, s, k).wait_recv()
+        self.beside(here, 1 - self.plane, s, k).start()
+
+    def step(self, number):
+        z, n = self.z, self.n
+        if number < len(self.steps):
+            d, k = self.steps[number]
+            pl.when(z >= d)(lambda: self.arrived(z - d, k, 0))
+            pl.when(z + d < n)(lambda: self.arrived(z + d, k, 1))
+        if 0 < number <= len(self.steps):
+            d, k = self.steps[number - 1]
+            pl.when(z >= d)(lambda: self.crossed(z - d, k))
+            pl.when(z + d < n)(lambda: self.crossed(z + d, k))
+
+    def whole(self, s):
+        for k in self.every:
+            for mod in range(2):
+                self.beside(self.place(mod, s, self.core, k), mod, s, k).wait_recv()
+                pl.when(s == self.z)(lambda: self.local(mod, k).wait())
+
+    def finish(self, s):
+        ways = neighbours()
+        for k in self.every:
+            here = self.place(self.plane, s, self.core, k)
+            pl.when(self.z != s)(lambda: self.across(here, self.plane, s, k).wait_send())
+            pl.when(ways[0][1] & (s <= self.z))(lambda: self.along(here, s, k, 0).wait_send())
+            pl.when(ways[1][1] & (s >= self.z))(lambda: self.along(here, s, k, 1).wait_send())
+            for mod in range(2):
+                self.beside(self.place(mod, s, self.core, k), mod, s, k).wait_send()
+
+
+def gather_kernel(count, pieces, firsts, *refs):
+    gather = Gather(pieces, firsts, refs[:count], refs[count : 2 * count], refs[2 * count :])
+    greet(neighbours())
+    gather.start()
+    for number in range(len(gather.steps) + 1):
+        gather.step(number)
+    for s in range(gather.n):
+        gather.whole(s)
+        gather.finish(s)
+
+
+def gather_semaphores(n, total):
+    shapes = [(n, total), (n, total), (2, n, total)] + [(n, total)] * 3 + [(2, n, total), (2, total)]
+    return [pltpu.SemaphoreType.DMA(shape) for shape in shapes]
+
+
+def attend_kernel(pieces, kv_local, *refs):
+    query, own_kv, w_shard, own_info, key_info, out = refs[:6]
+    kv, bias, attended, w_whole, outgoing, incoming, kept = refs[6:13]
+    kv_recv, kv_up, kv_down, kv_beside, kv_other, swap_send, swap_recv = refs[13:20]
+    gather = Gather(pieces, lambda which: 0, [w_shard], [w_whole], refs[20:])
+    n, z, core = gather.n, gather.z, gather.core
+    head = lax.axis_index("head")
+    length = own_kv.shape[0]
+    other = {"head": 1 - head}
+    ways = neighbours()
+    greet(ways + ((other, z >= 0),))
+
+    def rows(s, c):
+        return kv.at[pl.ds(pl.multiple_of((s * 2 + c) * length, 16), length)]
+
+    def along(src, s, way):
+        send = (kv_up, kv_down)[way]
+        return remote(src, rows(s, core), send.at[s], kv_recv.at[s], ways[way][0])
+
+    def beside(src, s):
+        return remote(src, rows(s, core), kv_beside.at[s], kv_other.at[s], ways[3][0])
+
+    for way in (0, 1):
+        pl.when(ways[way][1])(lambda: along(own_kv, z, way).start())
+    beside(own_kv, z).start()
+    gather.start()
+    kv[pl.ds(pl.multiple_of((z * 2 + core) * length, 16), length)] = own_kv[...]
+
+    own_doc, own_block, own_mod = [own_info[:, i : i + 1] for i in range(3)]
+    total = bias.shape[1]
+    query_pos = (z * 2 + core) * length + lax.broadcasted_iota(jnp.int32, (length, total), 0)
+    key_pos = lax.broadcasted_iota(jnp.int32, (length, total), 1)
+    seen = (own_doc == key_info[0:1, :]) & (
+        (key_pos <= query_pos) | ((own_block == key_info[1:2, :]) & (own_mod == 1))
+    )
+    bias[...] = jnp.where(seen, 0.0, -1e30)
+
+    def pass_on(s, way):
+        along(rows(s, core), s, way).wait_recv()
+        pl.when(ways[way][1])(lambda: along(rows(s, core), s, way).start())
+        beside(rows(s, core), s).start()
+
+    for d in range(1, n):
+        pl.when(z >= d)(lambda: pass_on(z - d, 0))
+        pl.when(z + d < n)(lambda: pass_on(z + d, 1))
+    for s in range(n):
+        beside(rows(s, core), s).wait_recv()
+
+    heads = query.shape[1] // HEAD_DIM
+    repeat = heads // kv_local
+    contract = (((1,), (1,)), ((), ()))
+
+    def attend(h):
+        columns = slice(h * HEAD_DIM, (h + 1) * HEAD_DIM)
+        first = h // repeat * HEAD_DIM
+        keys = kv[:, first : first + HEAD_DIM]
+        values = kv[:, kv_local * HEAD_DIM + first : kv_local * HEAD_DIM + first + HEAD_DIM]
+        scores = lax.dot_general(
+            query[:, columns], keys, contract, preferred_element_type=jnp.float32
+        )
+        scores = scores * (1.0 / math.sqrt(HEAD_DIM)) + bias[...]
+        weights = jnp.exp(scores - jnp.max(scores, axis=1, keepdims=True))
+        weight_sum = jnp.sum(weights, axis=1, keepdims=True)
+        summed = jnp.dot(
+            weights.astype(jnp.bfloat16), values, preferred_element_type=jnp.float32
+        )
+        attended[:, columns] = (summed / weight_sum).astype(jnp.bfloat16)
+
+    wide = outgoing.shape[2]
+    slots = outgoing.shape[0]
+
+    def swap(slot):
+        return remote(
+            outgoing.at[slot], incoming.at[slot], swap_send.at[slot], swap_recv.at[slot], other
+        )
+
+    def project(s):
+        gather.whole(s)
+        start = pl.multiple_of(s * wide, 16)
+        first, second = [
+            lax.dot_general(
+                attended[...],
+                w_whole[mod, pl.ds(start, wide), :],
+                contract,
+                preferred_element_type=jnp.float32,
+            )
+            for mod in range(2)
+        ]
+        partial = jnp.where(own_info[:, 2:3] == 1, second, first).astype(jnp.bfloat16)
+        slot = lax.rem(s, slots)
+        mine = lax.div(s, slots) == head
+
+        @pl.when(mine)
+        def _():
+            kept[slot] = partial
+
+        @pl.when(jnp.logical_not(mine))
+        def _():
+            outgoing[slot] = partial
+            swap(slot).start()
+
+    def project_where(condition):
+        def one(s, carry):
+            pl.when(condition(jnp.abs(s - z)))(lambda: project(s))
+            return carry
+
+        lax.fori_loop(0, n, one, 0)
+
+    early = (n - 2) * len(pieces)
+    for number in range(early + 1):
+        gather.step(number)
+        if number < heads:
+            attend(number)
+    for h in range(early + 1, heads):
+        attend(h)
+    project_where(lambda distance: distance < n - 1)
+    for number in range(early + 1, len(gather.steps) + 1):
+        gather.step(number)
+    project_where(lambda distance: distance == n - 1)
+
+    for slot in range(slots):
+        swap(slot).wait_recv()
+        out[:, slot * wide : (slot + 1) * wide] = (
+            kept[slot].astype(jnp.float32) + incoming[slot].astype(jnp.float32)
+        ).astype(out.dtype)
+    for s in range(n):
+        gather.finish(s)
+        beside(rows(s, core), s).wait_send()
+        pl.when(ways[0][1] & (s <= z))(lambda: along(rows(s, core), s, 0).wait_send())
+        pl.when(ways[1][1] & (s >= z))(lambda: along(rows(s, core), s, 1).wait_send())
+    for slot in range(slots):
+        swap(slot).wait_send()
+
+
+def attend_and_project(query, own_kv, w_shard, own_info, key_info, kv_local):
+    n = lax.axis_size("seq")
+    length, total = query.shape[0], key_info.shape[1]
+    _, shard, depth = w_shard.shape
+    pieces = [(0, *piece) for piece in cut(shard)]
+    half = n * shard
+    bf16 = jnp.bfloat16
+    sem = pltpu.SemaphoreType.DMA
+    any_space, vmem = pl.BlockSpec(memory_space=pl.ANY), pl.BlockSpec(memory_space=pltpu.VMEM)
+    return pl.pallas_call(
+        functools.partial(attend_kernel, pieces, kv_local),
+        out_shape=jax.ShapeDtypeStruct((length, half), bf16),
+        in_specs=[vmem, vmem, any_space, vmem, vmem],
+        out_specs=vmem,
+        scratch_shapes=[
+            pltpu.VMEM((total, own_kv.shape[1]), bf16),
+            pltpu.VMEM((length, total), jnp.float32),
+            pltpu.VMEM(query.shape, bf16),
+            pltpu.VMEM((2, 2 * half, depth), bf16),
+        ]
+        + [pltpu.VMEM((n // 2, length, 2 * shard), bf16)] * 3
+        + [sem((n,))] * 5
+        + [sem((n // 2,))] * 2
+        + gather_semaphores(n, len(pieces)),
+        compiler_params=pltpu.CompilerParams(
+            collective_id=1, has_side_effects=True, vmem_limit_bytes=52 * 2**20
+        ),
+        cost_estimate=pl.CostEstimate(
+            flops=4 * length * depth * (total + 2 * half),
+            bytes_accessed=64 * half * depth,
+            transcendentals=length * total * depth // HEAD_DIM,
+        ),
+    )(query, own_kv, w_shard, own_info, key_info)
+
+
+def gather_weights(shards, widths, firsts, collective_id):
+    n = lax.axis_size("seq")
+    if lax.axis_size("grp") != 2 or lax.axis_size("sub") != 2:
+        return [
+            lax.all_gather(
+                lax.dynamic_slice_in_dim(x, firsts(i), widths[i], 2), ("seq", "sub"), axis=1, tiled=True
+            )
+            for i, x in enumerate(shards)
+        ]
+    pieces = [(i, *piece) for i, x in enumerate(shards) for piece in cut(x.shape[1])]
+    total = len(pieces)
+    shapes = [
+        jax.ShapeDtypeStruct((2, 2 * n * x.shape[1], width), x.dtype)
+        for x, width in zip(shards, widths)
+    ]
+    moved = sum(2 * math.prod(shape.shape) for shape in shapes)
+    return pl.pallas_call(
+        functools.partial(gather_kernel, len(shards), pieces, firsts),
+        out_shape=shapes,
+        in_specs=[pl.BlockSpec(memory_space=pl.ANY)] * len(shards),
+        out_specs=[pl.BlockSpec(memory_space=pl.ANY)] * len(shards),
+        scratch_shapes=gather_semaphores(n, total),
+        compiler_params=pltpu.CompilerParams(collective_id=collective_id, has_side_effects=True),
+        cost_estimate=pl.CostEstimate(flops=0, bytes_accessed=8 * moved, transcendentals=0),
+    )(*shards)
 
 
 def body(tokens, norm_gain, w_query, w_key, w_value, w_out, modality, doc_ids):
     length = tokens.shape[0]
     head_count = lax.axis_size("head")
-    head_index = lax.axis_index("head")
     first_pos = lax.axis_index(("seq", "sub")) * length
     blocks = block_ids(modality, doc_ids)
     own_mod = lax.dynamic_slice_in_dim(modality, first_pos, length)
@@ -38,25 +373,37 @@
     own_block = lax.dynamic_slice_in_dim(blocks, first_pos, length)
     generate = (own_mod == 1)[:, None]
     kv_local = max(KV_HEADS // head_count, 1)
-    kv_first = head_index * KV_HEADS // head_count
-    key_cols = lax.dynamic_slice_in_dim(w_key, kv_first * HEAD_DIM, kv_local * HEAD_DIM, 2)
-    value_cols = lax.dynamic_slice_in_dim(w_value, kv_first * HEAD_DIM, kv_local * HEAD_DIM, 2)
     values32 = tokens.astype(jnp.float32)
     factor = lax.rsqrt(jnp.mean(values32 * values32, axis=1, keepdims=True) + EPS)
     gain = jnp.where(generate, norm_gain[1][None, :], norm_gain[0][None, :])
     normed = (values32 * factor * gain).astype(jnp.bfloat16)
-    key_value_weight = jnp.concatenate([key_cols, value_cols], axis=2)
-    kv_both = gather_weight(key_value_weight)
-    q_both = gather_weight(w_query)
-    out_both = gather_weight(jnp.swapaxes(w_out, 1, 2))
+    kv_width = kv_local * HEAD_DIM
+
+    def first_column(which):
+        if which == 2:
+            return 0
+        return pl.multiple_of(lax.axis_index("head") * KV_HEADS // head_count * HEAD_DIM, HEAD_DIM)
+
+    key_both, value_both, q_both = gather_weights(
+        [w_key, w_value, w_query], [kv_width, kv_width, w_query.shape[2]], first_column, 0
+    )
+    w_out = jnp.swapaxes(w_out, 1, 2)
 
     def project(both):
         first = jnp.dot(normed, both[0], preferred_element_type=jnp.float32)
         second = jnp.dot(normed, both[1], preferred_element_type=jnp.float32)
         return jnp.where(generate, second, first).astype(jnp.bfloat16)
 
-    stacked = project(kv_both)
+    stacked = jnp.concatenate([project(key_both), project(value_both)], axis=1)
     query = project(q_both)
+    sizes = [lax.axis_size(axis) for axis in ("grp", "head", "sub")]
+    if sizes == [2, 2, 2] and lax.axis_size("seq") % 2 == 0 and lax.axis_size("seq") <= 4:
+        own_info = jnp.stack([own_doc, own_block, own_mod], axis=1)
+        key_info = jnp.stack([doc_ids, blocks])
+        return attend_and_project(query, stacked, w_out, own_info, key_info, kv_local)
+
+    w_out, query = lax.optimization_barrier((w_out, query))
+    (out_both,) = gather_weights([w_out], [w_out.shape[2]], lambda which: 0, 1)
     q_local = query.shape[1] // HEAD_DIM
     repeat = q_local // kv_local
     grouped = query.reshape(length, kv_local, repeat, HEAD_DIM)

time: 386 us -> 255 us (0.66)
  waiting for transfers between devices: 299 us -> 0 us
  Pallas kernels: 0 us -> 233 us
  matrix products: 45.3 us -> 9.23 us
  between operations: 13.3 us -> 0.18 us
  other arithmetic: 15 us -> 3.52 us
  local copies, waits for them, and re-layouts: 12.6 us -> 5.68 us
    all_gather x4 -> x0, waiting for transfers between devices: 272 us -> none  [the longest x3 253 us: gather_weight(): whole = lax.all_gather(own, ('grp', 'seq', 'sub'), axis=0, tiled=True)]
    pallas_call x0 -> x2, Pallas kernels: none -> 233 us  [the longest x1 119 us: attend_and_project(): pl.pallas_call(functools.partial(attend_kernel, pieces, kv_local), out_sh...]
    dot_general x6 -> x0, matrix products: 31.9 us -> none  [the longest x2 10.3 us: visit(): jnp.einsum('grqk,kgd->grqd', probs, values_here, preferred_element_type=j...]
    reduce_scatter x1 -> x0, waiting for transfers between devices: 27.3 us -> none  [body(): lax.psum_scatter(partial_sum.astype(jnp.bfloat16), 'head', scatter_dimens...]
    reduce_sum x2 -> x0, other arithmetic: 9.65 us -> none  [visit(): weight_sum = weight_sum * scaling + jnp.sum(weights, axis=3)]
    dynamic_slice x7 -> x0, local copies, waits for them, and re-layouts: 4.62 us -> none  [the longest x2 3.25 us: gather_weight(): lax.dynamic_index_in_dim(shard, lax.axis_index('grp'), 0, keepdims=False)]
    dot_general x2 -> x3, matrix products: 9.26 us -> 5.42 us  [project(): first = jnp.dot(normed, both[0], preferred_element_type=jnp.float32)]
  transfers between devices with their start and end apart: 5 -> 0, of which waited for: 5 -> 0; matrix products, arithmetic and copies ran while one was open for 14% -> 0% of each run, Pallas kernels for 0% -> 0%
where the time goes in v3:
time: 255 us; the launch traced here: 252 us
  Pallas kernels  233 us (91%)
  matrix products  9.23 us (4%)
  local copies, waits for them, and re-layouts  5.68 us (2%)
  other arithmetic  3.52 us (1%)
    pallas_call x1, Pallas kernels, attend_and_project(): pl.pallas_call(functools.partial(attend_kernel, pieces, kv_local), out_sh...  119 us
    pallas_call x1, Pallas kernels, gather_weights(): pl.pallas_call(functools.partial(gather_kernel, len(shards), pieces, firs...  114 us
    dot_general x3, matrix products, project(): first = jnp.dot(normed, both[0], preferred_element_type=jnp.float32)  5.42 us

profile of v3, /device:TPU:0, one launch (start us, length us, event | category | flops | bytes accessed | tf_op | source)
XLA Modules:
  0.0 251.8 jit_solution(17862887412668956818)
XLA Ops:
  0.0 0.0 copy-start
  0.0 0.9 broadcast_compare_fusion
  0.9 0.9 slice_reduce_fusion.1
  1.8 1.9 fusion.6
  3.8 114.1 %shard_map.82 = (bf16[2,3584,256]{2,1,0:T(8,128)(2,1)}, bf16[2,3584,256]{2,1,0:T(8,128)(2,1)}, bf16[2,3584,1024]{2,1,0:T(8,128)(2,1)}) custom-call(bf16[2,448,512]{2,1,0:T(8,128)(2,1)} %refs_0_.1, bf16[2,448,512]{2,1,0:T(8,128)(2,1)} %refs_1_.1, bf16[2,448,1024]{2,1,0:T(8,128)(2,1)} %refs_2_.1), custom_call_target="tpu_custom_call" | custom-call | bytes 176160768 | tf_op jit(solution)/shard_map/pallas_call | solution.py:355
  117.9 0.0 copy-done
  117.9 0.0 copy-start.4
  117.9 0.0 slice-start
  117.9 2.4 fusion.13
  120.3 0.2 copy-done.4
  120.5 0.0 copy-start.3
  120.5 0.0 slice-start.1
  120.5 0.8 fusion.36
  121.2 1.5 copy-done.3
  122.8 0.0 slice-start.2
  122.8 0.8 fusion.9
  123.5 0.0 slice-start.3
  123.6 0.8 fusion.33
  124.4 0.0 slice-done
  124.4 0.0 slice-done.1
  124.4 1.0 slice-done.2
  125.4 0.7 slice-done.3
  126.1 2.2 fusion
  128.3 0.0 copy-start.1
  128.3 0.0 copy-start.2
  128.3 2.2 fusion.24.refs_0_
  130.6 0.0 copy-done.1
  130.6 0.0 copy-done.2
  130.6 0.1 fusion.39
  130.7 0.1 convert_bitcast_fusion
  130.8 0.3 reduce-window.9
  131.1 0.1 slice.57
  131.2 0.1 slice_reduce_fusion.2
  131.3 0.1 fusion.46
  131.4 0.1 dynamic_slice.11
  131.4 0.1 dynamic_slice.10
  131.5 0.1 copy.24.refs_3_
  131.7 0.1 broadcast_add_fusion
  131.8 119.1 %shard_map.83 = bf16[256,1792]{1,0:T(8,128)(2,1)S(1)} custom-call(bf16[256,1024]{1,0:T(8,128)(2,1)S(1)} %fusion.24.refs_0_, bf16[256,512]{1,0:T(8,128)(2,1)S(1)} %pad_maximum_fusion.refs_1_, bf16[2,448,1024]{2,1,0:T(8,128)(2,1)} %bitcast.47, s32[256,3]{1,0:T(8,128)S(1)} %copy.24.refs_3_, s32[2,2048]{1,0:T(2,128)S(1)} %pad_add_fusion.refs_4_), custom_call_target="tpu_custom_call" | custom-call | flops 5905580032 | bytes 117440512 | tf_op jit(solution)/shard_map/pallas_call | solution.py:313
  250.9 0.9 copy.30
  (6 shorter events, 0.1 us)
Async XLA Ops:
  0.0 117.9 %copy-start = (bf16[256,3584]{1,0:T(8,128)(2,1)S(1)}, bf16[256,3584]{1,0:T(8,128)(2,1)}, u32[]{:S(2)}) copy-start(bf16[256,3584]{1,0:T(8,128)(2,1)} %param.8) | copy-start | bytes 5505028
  117.9 2.6 %copy-start.4 = (bf16[2,3584,256]{2,1,0:T(8,128)(2,1)S(1)}, bf16[2,3584,256]{2,1,0:T(8,128)(2,1)}, u32[]{:S(2)}) copy-start(bf16[2,3584,256]{2,1,0:T(8,128)(2,1)} %get-tuple-element.9) | copy-start | bytes 11010052
  117.9 6.5 %slice-start = ((s8[14680064]{0:T(1024)(128)(4,1)}), s8[4194304]{0:T(1024)(128)(4,1)S(1)}, s32[]{:S(2)}) async-start(s8[14680064]{0:T(1024)(128)(4,1)} %bitcast.45), calls=%async_computation | async-start | bytes 8388608
  120.5 2.3 copy-start.3
  120.5 3.9 %slice-start.1 = ((s8[14680064]{0:T(1024)(128)(4,1)}), s8[4194304]{0:T(1024)(128)(4,1)S(1)}, s32[]{:S(2)}) async-start(s8[14680064]{0:T(1024)(128)(4,1)} %bitcast.45), calls=%async_computation.1 | async-start | bytes 8388608
  122.8 2.6 %slice-start.2 = ((s8[14680064]{0:T(1024)(128)(4,1)}), s8[4194304]{0:T(1024)(128)(4,1)S(1)}, s32[]{:S(2)}) async-start(s8[14680064]{0:T(1024)(128)(4,1)} %bitcast.45), calls=%async_computation.2 | async-start | bytes 8388608
  123.5 2.5 slice-start.3
  128.3 2.3 copy-start.1
  128.3 2.3 copy-start.2

commit v4 on v3

--- a/solution.py
+++ b/solution.py
@@ -97,7 +97,7 @@
         dst = self.place(mod, self.z, self.core, k)
         return pltpu.make_async_copy(self.own(mod, k), dst, self.semaphores[7].at[mod, k])
 
-    def start(self):
+    def start_along(self):
         ways = neighbours()
         for k in self.every:
             for way in (0, 1):
@@ -106,6 +106,8 @@
                     self.along(self.own(self.plane, k), self.z, k, way).start()
 
                 pl.when(ways[way][1])(send)
+
+    def start_beside(self):
         for k in self.every:
             for mod in range(2):
                 self.beside(self.own(mod, k), mod, self.z, k).start()
@@ -123,16 +125,26 @@
         self.across(here, 1 - self.plane, s, k).wait_recv()
         self.beside(here, 1 - self.plane, s, k).start()
 
-    def step(self, number):
+    def step(self, d, k):
         z, n = self.z, self.n
-        if number < len(self.steps):
-            d, k = self.steps[number]
-            pl.when(z >= d)(lambda: self.arrived(z - d, k, 0))
-            pl.when(z + d < n)(lambda: self.arrived(z + d, k, 1))
-        if 0 < number <= len(self.steps):
-            d, k = self.steps[number - 1]
-            pl.when(z >= d)(lambda: self.crossed(z - d, k))
-            pl.when(z + d < n)(lambda: self.crossed(z + d, k))
+        pl.when(z >= d)(lambda: self.arrived(z - d, k, 0))
+        pl.when(z + d < n)(lambda: self.arrived(z + d, k, 1))
+        if d < n - 1:
+            self.cross(d - 1, k)
+        else:
+            for late in (2 * k, 2 * k + 1):
+                self.cross(d - 1, late)
+            self.cross(d, k - 2)
+
+    def cross(self, d, k):
+        if d > 0 and 0 <= k < len(self.pieces):
+            pl.when(self.z >= d)(lambda: self.crossed(self.z - d, k))
+            pl.when(self.z + d < self.n)(lambda: self.crossed(self.z + d, k))
+
+    def last_cross(self):
+        total = len(self.pieces)
+        for k in range(max(total - 2, 0), total):
+            self.cross(self.n - 1, k)
 
     def whole(self, s):
         for k in self.every:
@@ -154,9 +166,11 @@
 def gather_kernel(count, pieces, firsts, *refs):
     gather = Gather(pieces, firsts, refs[:count], refs[count : 2 * count], refs[2 * count :])
     greet(neighbours())
-    gather.start()
-    for number in range(len(gather.steps) + 1):
-        gather.step(number)
+    gather.start_along()
+    gather.start_beside()
+    for d, k in gather.steps:
+        gather.step(d, k)
+    gather.last_cross()
     for s in range(gather.n):
         gather.whole(s)
         gather.finish(s)
@@ -192,7 +206,7 @@
     for way in (0, 1):
         pl.when(ways[way][1])(lambda: along(own_kv, z, way).start())
     beside(own_kv, z).start()
-    gather.start()
+    gather.start_beside()
     kv[pl.ds(pl.multiple_of((z * 2 + core) * length, 16), length)] = own_kv[...]
 
     own_doc, own_block, own_mod = [own_info[:, i : i + 1] for i in range(3)]
@@ -212,6 +226,7 @@
     for d in range(1, n):
         pl.when(z >= d)(lambda: pass_on(z - d, 0))
         pl.when(z + d < n)(lambda: pass_on(z + d, 1))
+    gather.start_along()
     for s in range(n):
         beside(rows(s, core), s).wait_recv()
 
@@ -275,16 +290,21 @@
 
         lax.fori_loop(0, n, one, 0)
 
-    early = (n - 2) * len(pieces)
-    for number in range(early + 1):
-        gather.step(number)
+    early = [step for step in gather.steps if step[0] < n - 1]
+    for number, step in enumerate(early):
+        gather.step(*step)
         if number < heads:
             attend(number)
-    for h in range(early + 1, heads):
+    for h in range(len(early), heads):
         attend(h)
-    project_where(lambda distance: distance < n - 1)
-    for number in range(early + 1, len(gather.steps) + 1):
-        gather.step(number)
+    project_where(lambda distance: distance < n - 2)
+    crossed_by = (len(pieces) + 1) // 2
+    for k in range(crossed_by):
+        gather.step(n - 1, k)
+    project_where(lambda distance: distance == n - 2)
+    for k in range(crossed_by, len(pieces)):
+        gather.step(n - 1, k)
+    gather.last_cross()
     project_where(lambda distance: distance == n - 1)
 
     for slot in range(slots):

time: 255 us -> 230 us (0.902)
  Pallas kernels: 233 us -> 210 us
    pallas_call x1, Pallas kernels: 119 us -> 103 us  [attend_and_project(): pl.pallas_call(functools.partial(attend_kernel, pieces, kv_local), out_sh...]
    pallas_call x1, Pallas kernels: 114 us -> 107 us  [gather_weights(): pl.pallas_call(functools.partial(gather_kernel, len(shards), pieces, firs...]
where the time goes in v4:
time: 230 us; the launch traced here: 229 us
  Pallas kernels  210 us (91%)
  matrix products  9.23 us (4%)
  local copies, waits for them, and re-layouts  5.68 us (2%)
  other arithmetic  3.52 us (2%)
    pallas_call x1, Pallas kernels, gather_weights(): pl.pallas_call(functools.partial(gather_kernel, len(shards), pieces, firs...  107 us
    pallas_call x1, Pallas kernels, attend_and_project(): pl.pallas_call(functools.partial(attend_kernel, pieces, kv_local), out_sh...  103 us
    dot_general x3, matrix products, project(): first = jnp.dot(normed, both[0], preferred_element_type=jnp.float32)  5.42 us

profile of v4, /device:TPU:0, one launch (start us, length us, event | category | flops | bytes accessed | tf_op | source)
XLA Modules:
  0.0 228.8 jit_solution(18445858521342815031)
XLA Ops:
  0.0 0.0 copy-start
  0.0 0.9 broadcast_compare_fusion
  0.9 0.9 slice_reduce_fusion.1
  1.8 1.9 fusion.6
  3.8 107.3 %shard_map.82 = (bf16[2,3584,256]{2,1,0:T(8,128)(2,1)}, bf16[2,3584,256]{2,1,0:T(8,128)(2,1)}, bf16[2,3584,1024]{2,1,0:T(8,128)(2,1)}) custom-call(bf16[2,448,512]{2,1,0:T(8,128)(2,1)} %refs_0_.1, bf16[2,448,512]{2,1,0:T(8,128)(2,1)} %refs_1_.1, bf16[2,448,1024]{2,1,0:T(8,128)(2,1)} %refs_2_.1), custom_call_target="tpu_custom_call" | custom-call | bytes 176160768 | tf_op jit(solution)/shard_map/pallas_call | solution.py:375
  111.1 0.0 copy-done
  111.1 0.0 copy-start.4
  111.1 0.0 slice-start
  111.1 2.4 %fusion.13 = bf16[256,256]{1,0:T(8,128)(2,1)S(1)} fusion(bf16[2,3584,256]{2,1,0:T(8,128)(2,1)} %get-tuple-element.9, bf16[256,3584]{1,0:T(8,128)(2,1)S(1)} %copy-done, f32[3584]{0:T(1024)S(1)} %get-tuple-element.12, f32[3584]{0:T(1024)S(1)} %get-tuple-element.11, f32[256]{0:T(256)S(1)} %add_rsqrt_fusion, pred[256]{0:T(512)(128)(4,1)S(1)} %get-tuple-element.13), kind=kOutput, calls=%fused_computation.15 | convolution fusion | flops 474349568 | bytes 3831040 | tf_op jit(solution)/shard_map/dot_general | solution.py:413
  113.5 0.2 copy-done.4
  113.7 0.0 copy-start.3
  113.7 0.0 slice-start.1
  113.7 0.8 fusion.36
  114.4 1.5 copy-done.3
  116.0 0.0 slice-start.2
  116.0 0.8 fusion.9
  116.7 0.0 slice-start.3
  116.7 0.8 fusion.33
  117.6 0.0 slice-done
  117.6 0.0 slice-done.1
  117.6 1.0 slice-done.2
  118.6 0.7 slice-done.3
  119.3 2.2 fusion
  121.5 0.0 copy-start.1
  121.5 0.0 copy-start.2
  121.5 2.2 fusion.24.refs_0_
  123.8 0.0 copy-done.1
  123.8 0.0 copy-done.2
  123.8 0.1 fusion.39
  123.9 0.1 convert_bitcast_fusion
  124.0 0.3 reduce-window.9
  124.2 0.1 slice.57
  124.4 0.1 slice_reduce_fusion.2
  124.5 0.1 fusion.46
  124.5 0.1 dynamic_slice.11
  124.6 0.1 dynamic_slice.10
  124.7 0.1 copy.24.refs_3_
  124.9 0.1 broadcast_add_fusion
  125.0 102.9 %shard_map.83 = bf16[256,1792]{1,0:T(8,128)(2,1)S(1)} custom-call(bf16[256,1024]{1,0:T(8,128)(2,1)S(1)} %fusion.24.refs_0_, bf16[256,512]{1,0:T(8,128)(2,1)S(1)} %pad_maximum_fusion.refs_1_, bf16[2,448,1024]{2,1,0:T(8,128)(2,1)} %bitcast.47, s32[256,3]{1,0:T(8,128)S(1)} %copy.24.refs_3_, s32[2,2048]{1,0:T(2,128)S(1)} %pad_add_fusion.refs_4_), custom_call_target="tpu_custom_call" | custom-call | flops 5905580032 | bytes 117440512 | tf_op jit(solution)/shard_map/pallas_call | solution.py:333
  227.9 0.9 copy.30
  (6 shorter events, 0.1 us)
Async XLA Ops:
  0.0 111.1 %copy-start = (bf16[256,3584]{1,0:T(8,128)(2,1)S(1)}, bf16[256,3584]{1,0:T(8,128)(2,1)}, u32[]{:S(2)}) copy-start(bf16[256,3584]{1,0:T(8,128)(2,1)} %param.8) | copy-start | bytes 5505028
  111.1 2.6 %copy-start.4 = (bf16[2,3584,256]{2,1,0:T(8,128)(2,1)S(1)}, bf16[2,3584,256]{2,1,0:T(8,128)(2,1)}, u32[]{:S(2)}) copy-start(bf16[2,3584,256]{2,1,0:T(8,128)(2,1)} %get-tuple-element.9) | copy-start | bytes 11010052
  111.1 6.5 %slice-start = ((s8[14680064]{0:T(1024)(128)(4,1)}), s8[4194304]{0:T(1024)(128)(4,1)S(1)}, s32[]{:S(2)}) async-start(s8[14680064]{0:T(1024)(128)(4,1)} %bitcast.45), calls=%async_computation | async-start | bytes 8388608
  113.7 2.3 %copy-start.3 = (bf16[2,3584,256]{2,1,0:T(8,128)(2,1)S(1)}, bf16[2,3584,256]{2,1,0:T(8,128)(2,1)}, u32[]{:S(2)}) copy-start(bf16[2,3584,256]{2,1,0:T(8,128)(2,1)} %get-tuple-element.10) | copy-start | bytes 11010052
  113.7 3.9 %slice-start.1 = ((s8[14680064]{0:T(1024)(128)(4,1)}), s8[4194304]{0:T(1024)(128)(4,1)S(1)}, s32[]{:S(2)}) async-start(s8[14680064]{0:T(1024)(128)(4,1)} %bitcast.45), calls=%async_computation.1 | async-start | bytes 8388608
  116.0 2.6 %slice-start.2 = ((s8[14680064]{0:T(1024)(128)(4,1)}), s8[4194304]{0:T(1024)(128)(4,1)S(1)}, s32[]{:S(2)}) async-start(s8[14680064]{0:T(1024)(128)(4,1)} %bitcast.45), calls=%async_computation.2 | async-start | bytes 8388608
  116.7 2.5 %slice-start.3 = ((s8[14680064]{0:T(1024)(128)(4,1)}), s8[2097152]{0:T(1024)(128)(4,1)S(1)}, s32[]{:S(2)}) async-start(s8[14680064]{0:T(1024)(128)(4,1)} %bitcast.45), calls=%async_computation.3 | async-start | bytes 4194304
  121.5 2.3 copy-start.1
  121.5 2.3 copy-start.2

commit v5 on v4

--- a/solution.py
+++ b/solution.py
@@ -182,10 +182,12 @@
 
 
 def attend_kernel(pieces, kv_local, *refs):
-    query, own_kv, w_shard, own_info, key_info, out = refs[:6]
-    kv, bias, attended, w_whole, outgoing, incoming, kept = refs[6:13]
-    kv_recv, kv_up, kv_down, kv_beside, kv_other, swap_send, swap_recv = refs[13:20]
-    gather = Gather(pieces, lambda which: 0, [w_shard], [w_whole], refs[20:])
+    normed, w_query, own_kv, w_shard, own_info, key_info, out = refs[:7]
+    w_near, query, kv, bias, attended, w_whole, outgoing, incoming, kept = refs[7:16]
+    near, kv_recv, kv_up, kv_down, kv_beside, kv_other, swap_send, swap_recv = refs[16:24]
+    gather = Gather(pieces, lambda which: 0, [w_shard], [w_whole], refs[24:])
+    bring = pltpu.make_async_copy(w_query, w_near, near)
+    bring.start()
     n, z, core = gather.n, gather.z, gather.core
     head = lax.axis_index("head")
     length = own_kv.shape[0]
@@ -223,10 +225,24 @@
         pl.when(ways[way][1])(lambda: along(rows(s, core), s, way).start())
         beside(rows(s, core), s).start()
 
+    def ask(part):
+        columns = slice(part * query.shape[1] // 2, (part + 1) * query.shape[1] // 2)
+        first, second = [
+            jnp.dot(normed[...], w_near[mod, :, columns], preferred_element_type=jnp.float32)
+            for mod in range(2)
+        ]
+        query[:, columns] = jnp.where(own_mod == 1, second, first).astype(jnp.bfloat16)
+
     for d in range(1, n):
         pl.when(z >= d)(lambda: pass_on(z - d, 0))
         pl.when(z + d < n)(lambda: pass_on(z + d, 1))
-    gather.start_along()
+        if d == n - 1:
+            gather.start_along()
+        if d == 1:
+            bring.wait()
+            ask(0)
+        if d == min(2, n - 1):
+            ask(1)
     for s in range(n):
         beside(rows(s, core), s).wait_recv()
 
@@ -321,9 +337,9 @@
         swap(slot).wait_send()
 
 
-def attend_and_project(query, own_kv, w_shard, own_info, key_info, kv_local):
+def attend_and_project(normed, w_query, own_kv, w_shard, own_info, key_info, kv_local):
     n = lax.axis_size("seq")
-    length, total = query.shape[0], key_info.shape[1]
+    length, total = normed.shape[0], key_info.shape[1]
     _, shard, depth = w_shard.shape
     pieces = [(0, *piece) for piece in cut(shard)]
     half = n * shard
@@ -333,27 +349,30 @@
     return pl.pallas_call(
         functools.partial(attend_kernel, pieces, kv_local),
         out_shape=jax.ShapeDtypeStruct((length, half), bf16),
-        in_specs=[vmem, vmem, any_space, vmem, vmem],
+        in_specs=[vmem, any_space, vmem, any_space, vmem, vmem],
         out_specs=vmem,
         scratch_shapes=[
+            pltpu.VMEM(w_query.shape, bf16),
+            pltpu.VMEM((length, w_query.shape[2]), bf16),
             pltpu.VMEM((total, own_kv.shape[1]), bf16),
             pltpu.VMEM((length, total), jnp.float32),
-            pltpu.VMEM(query.shape, bf16),
+            pltpu.VMEM((length, w_query.shape[2]), bf16),
             pltpu.VMEM((2, 2 * half, depth), bf16),
         ]
         + [pltpu.VMEM((n // 2, length, 2 * shard), bf16)] * 3
+        + [sem]
         + [sem((n,))] * 5
         + [sem((n // 2,))] * 2
         + gather_semaphores(n, len(pieces)),
         compiler_params=pltpu.CompilerParams(
-            collective_id=1, has_side_effects=True, vmem_limit_bytes=52 * 2**20
+            collective_id=1, has_side_effects=True, vmem_limit_bytes=58 * 2**20
         ),
         cost_estimate=pl.CostEstimate(
             flops=4 * length * depth * (total + 2 * half),
             bytes_accessed=64 * half * depth,
             transcendentals=length * total * depth // HEAD_DIM,
         ),
-    )(query, own_kv, w_shard, own_info, key_info)
+    )(normed, w_query, own_kv, w_shard, own_info, key_info)
 
 
 def gather_weights(shards, widths, firsts, collective_id):
@@ -415,13 +434,13 @@
         return jnp.where(generate, second, first).astype(jnp.bfloat16)
 
     stacked = jnp.concatenate([project(key_both), project(value_both)], axis=1)
-    query = project(q_both)
     sizes = [lax.axis_size(axis) for axis in ("grp", "head", "sub")]
     if sizes == [2, 2, 2] and lax.axis_size("seq") % 2 == 0 and lax.axis_size("seq") <= 4:
         own_info = jnp.stack([own_doc, own_block, own_mod], axis=1)
         key_info = jnp.stack([doc_ids, blocks])
-        return attend_and_project(query, stacked, w_out, own_info, key_info, kv_local)
-
+        return attend_and_project(normed, q_both, stacked, w_out, own_info, key_info, kv_local)
+
+    query = project(q_both)
     w_out, query = lax.optimization_barrier((w_out, query))
     (out_both,) = gather_weights([w_out], [w_out.shape[2]], lambda which: 0, 1)
     q_local = query.shape[1] // HEAD_DIM

time: 230 us -> 230 us (level)
  matrix products: 9.23 us -> 4.2 us
  other arithmetic: 3.52 us -> 6.85 us
  Pallas kernels: 210 us -> 213 us
    dot_general x3 -> x2, matrix products: 3.81 us -> 1.28 us  [project(): second = jnp.dot(normed, both[1], preferred_element_type=jnp.float32)]
    dot_general x3 -> x2, matrix products: 5.42 us -> 2.92 us  [project(): first = jnp.dot(normed, both[0], preferred_element_type=jnp.float32)]
    pallas_call x1, Pallas kernels: 103 us -> 105 us  [attend_and_project(): pl.pallas_call(functools.partial(attend_kernel, pieces, kv_local), out_sh...]
where the time goes in v5:
time: 230 us
  Pallas kernels  213 us (93%)
  other arithmetic  6.85 us (3%)
  local copies, waits for them, and re-layouts  5.91 us (3%)
  matrix products  4.2 us (2%)
    pallas_call x1, Pallas kernels, gather_weights(): pl.pallas_call(functools.partial(gather_kernel, len(shards), pieces, firs...  107 us
    pallas_call x1, Pallas kernels, attend_and_project(): pl.pallas_call(functools.partial(attend_kernel, pieces, kv_local), out_sh...  105 us

profile of v5, /device:TPU:0, one launch (start us, length us, event | category | flops | bytes accessed | tf_op | source)
XLA Modules:
  0.0 229.7 jit_solution(14461930039773666736)
XLA Ops:
  0.0 0.0 copy-start
  0.0 0.9 broadcast_compare_fusion
  0.9 0.9 slice_reduce_fusion.1
  1.8 1.9 fusion
  3.8 0.0 copy-done
  3.8 2.0 fusion.2.refs_0_
  5.8 0.0 copy-start.1
  5.8 107.2 %shard_map.82 = (bf16[2,3584,256]{2,1,0:T(8,128)(2,1)}, bf16[2,3584,256]{2,1,0:T(8,128)(2,1)}, bf16[2,3584,1024]{2,1,0:T(8,128)(2,1)}) custom-call(bf16[2,448,512]{2,1,0:T(8,128)(2,1)} %refs_0_.1, bf16[2,448,512]{2,1,0:T(8,128)(2,1)} %refs_1_.1, bf16[2,448,1024]{2,1,0:T(8,128)(2,1)} %refs_2_.1), custom_call_target="tpu_custom_call" | custom-call | bytes 176160768 | tf_op jit(solution)/shard_map/pallas_call | solution.py:394
  113.0 0.0 copy-done.1
  113.0 0.0 copy-start.5
  113.0 2.3 fusion.7
  115.3 0.3 copy-done.5
  115.6 0.0 copy-start.4
  115.6 0.6 fusion.24
  116.3 1.4 copy-done.4
  117.7 0.6 fusion.3
  118.3 0.0 copy-start.2
  118.3 0.0 copy-start.3
  118.3 0.6 fusion.21
  119.0 0.7 pad_maximum_fusion.refs_2_
  119.7 0.0 copy-done.2
  119.7 0.0 copy-done.3
  119.7 0.1 fusion.27
  119.8 0.1 convert_bitcast_fusion
  119.9 0.3 reduce-window.9
  120.2 0.1 slice.49
  120.3 0.1 slice_reduce_fusion.2
  120.4 0.1 fusion.32
  120.5 0.1 dynamic_slice.11
  120.5 0.1 dynamic_slice.10
  120.6 0.8 copy.24.refs_4_
  121.4 0.1 broadcast_add_fusion
  121.5 0.6 pad_add_fusion.refs_5_
  122.1 105.4 %shard_map.83 = bf16[256,1792]{1,0:T(8,128)(2,1)} custom-call(bf16[256,3584]{1,0:T(8,128)(2,1)} %fusion.2.refs_0_, bf16[2,3584,1024]{2,1,0:T(8,128)(2,1)} %get-tuple-element.8.refs_1_, bf16[256,512]{1,0:T(8,128)(2,1)} %pad_maximum_fusion.refs_2_, bf16[2,448,1024]{2,1,0:T(8,128)(2,1)} %bitcast.39, s32[256,3]{1,0:T(8,128)} %copy.24.refs_4_, ...), custom_call_target="tpu_custom_call" | custom-call | flops 5905580032 | bytes 117440512 | tf_op jit(solution)/shard_map/pallas_call | solution.py:349
  227.5 2.2 copy.30
  (3 shorter events, 0.1 us)
Async XLA Ops:
  0.0 3.8 %copy-start = (bf16[256,3584]{1,0:T(8,128)(2,1)S(1)}, bf16[256,3584]{1,0:T(8,128)(2,1)}, u32[]{:S(2)}) copy-start(bf16[256,3584]{1,0:T(8,128)(2,1)} %param.8) | copy-start | bytes 5505028
  5.8 107.2 %copy-start.1 = (bf16[256,3584]{1,0:T(8,128)(2,1)S(1)}, bf16[256,3584]{1,0:T(8,128)(2,1)}, u32[]{:S(2)}) copy-start(bf16[256,3584]{1,0:T(8,128)(2,1)} %fusion.2.refs_0_) | copy-start | bytes 5505028
  113.0 2.6 %copy-start.5 = (bf16[2,3584,256]{2,1,0:T(8,128)(2,1)S(1)}, bf16[2,3584,256]{2,1,0:T(8,128)(2,1)}, u32[]{:S(2)}) copy-start(bf16[2,3584,256]{2,1,0:T(8,128)(2,1)} %get-tuple-element.9) | copy-start | bytes 11010052
  115.6 2.0 copy-start.4
  118.3 1.4 copy-start.2
  118.3 1.4 copy-start.3
